TPU v7x, 128 devices: a whole 4x4x4 slice. The times are simulated.
128 devices in a mesh: row: 8 (over x, core), col: 16 (over y, z).
Axes of the slice: x: 4, y: 4, z: 4, core: 2. Of those that a mesh axis runs over, the one named last changes fastest.
Arguments:
- embeddings: float32 [65536, 1024], P(('row', 'col')), may hold values from -6 to 6
- dest_pos: int32 [65536], P(('row', 'col')), may hold values from 0 to 65535, as said below
- cluster_ids: int32 [8, 8192], P('row', 'col'), may hold values from 0 to 15, as said below
Outputs:
- best_match: float32 [8, 8192], P('row', 'col')
Inputs may be any that keep to these rules, and one draw needn't show every extreme that they name: dest_pos is a permutation; of the 512 rows stored on one device at most 8 have positions in one device's block of 512 positions, and exactly 8 for some pairs of devices. In each group cluster_ids never falls along the positions; every cluster holds 200 to 5120 positions, and one cluster of each group exactly 5120.
All inputs are finite; a program needn't handle non-finite values.
Results may differ from a plain program's by a relative error of at most 0.0013.
Values may be sent and summed in bfloat16 or wider, within the bound.
A program may use at most 64 MiB of HBM per device.

v0:
```python
import jax
import jax.numpy as jnp
from jax import lax
from jax.sharding import PartitionSpec as P


def normalize(rows):
    scale = lax.rsqrt(jnp.sum(rows * rows, axis=1, keepdims=True) + 1e-06)
    return (rows * scale).astype(jnp.bfloat16)


def masked_sims(left, left_labels, right, right_labels, keep_extra):
    sims = lax.dot_general(
        left, right, (((1,), (1,)), ((), ())), preferred_element_type=jnp.float32
    )
    keep = (left_labels[:, None] == right_labels[None, :]) & keep_extra
    return jnp.where(keep, sims, jnp.float32(-1.0))


def shards(embeddings, dest_pos, cluster_ids):
    rows_dev, width = embeddings.shape
    devs = lax.axis_size("row") * lax.axis_size("col")
    slots = max(4, 2 * rows_dev // devs)
    unit = normalize(embeddings)
    target = dest_pos // rows_dev
    place = dest_pos % rows_dev
    onehot = (target[:, None] == jnp.arange(devs, dtype=jnp.int32)[None, :]).astype(jnp.int32)
    slot = jnp.sum(jnp.cumsum(onehot, axis=0) * onehot, axis=1) - 1
    send_rows = jnp.zeros((devs, slots, width), jnp.bfloat16).at[target, slot].set(unit)
    send_places = jnp.full((devs, slots), rows_dev, jnp.int32).at[target, slot].set(place)
    got_rows, got_places = (
        lax.all_to_all(send_rows, ("row", "col"), split_axis=0, concat_axis=0, tiled=True),
        lax.all_to_all(send_places, ("row", "col"), split_axis=0, concat_axis=0, tiled=True),
    )
    mine = (
        jnp.zeros((rows_dev, width), jnp.bfloat16)
        .at[got_places.reshape(-1)]
        .set(got_rows.reshape(-1, width), mode="drop")
    )
    labels = cluster_ids.reshape(rows_dev)
    local_index = jnp.arange(rows_dev, dtype=jnp.int32)
    my_start = lax.axis_index("col") * rows_dev
    my_places = my_start + local_index
    init = jnp.full((rows_dev,), -1.0, jnp.float32)
    other = lax.all_gather(mine, "col", axis=0, tiled=True)
    other_labels = lax.all_gather(labels, "col", axis=0, tiled=True)
    columns = jnp.arange(other.shape[0], dtype=jnp.int32)
    sims = masked_sims(mine, labels, other, other_labels, my_places[:, None] != columns[None, :])
    best = jnp.maximum(init, jnp.max(sims, axis=1))
    return best.reshape(1, rows_dev)


def solution(mesh):
    return jax.shard_map(
        shards,
        mesh=mesh,
        in_specs=(P(("row", "col"), None), P(("row", "col")), P("row", "col")),
        out_specs=P("row", "col"),
        check_vma=False,
    )
```

profile of v0, /device:TPU:1, one launch (start us, length us, event | category | flops | bytes accessed | tf_op | source)
XLA Modules:
  0.0 291.5 jit_solution(7586716987220813444)
XLA Ops:
  6.5 0.7 compare_select_fusion.2
  7.2 0.1 copy.7
  7.3 0.2 fusion.5
  7.7 0.2 fusion.4
  7.9 0.0 copy-start
  7.9 22.0 %scatter_fusion = s32[128,8]{0,1:T(8,128)S(1)} fusion(s32[128,8]{0,1:T(8,128)S(1)} %broadcast_in_dim.14, s32[512]{0:T(512)S(1)} %bitcast.30, s32[512]{0:T(512)S(1)} %get-tuple-element.7), kind=kCustom, calls=%fused_computation | custom fusion | bytes 10240 | tf_op jit(solution)/shard_map/scatter | solution.py:30
  29.9 0.7 copy.9
  30.7 11.5 %all-to-all-start = ((s32[128,1,8]{2,1,0:T(1,128)}), s32[128,1,8]{2,1,0:T(1,128)S(1)}, u32[]{:S(2)}, u32[]{:S(2)}) async-start(s32[128,1,8]{2,1,0:T(1,128)} %copy.9), calls=%async_computation | async-start | bytes 131072 | tf_op jit(solution)/shard_map/all_to_all | solution.py:33
  42.2 0.0 copy-done
  42.2 0.2 multiply_reduce_fusion
  42.4 0.2 multiply_convert_fusion
  42.6 1.6 broadcast_in_dim.32
  44.2 71.8 %scatter_fusion.1 = bf16[128,8,1024]{2,1,0:T(8,128)(2,1)} fusion(bf16[128,8,1024]{2,1,0:T(8,128)(2,1)} %broadcast_in_dim.32, s32[512]{0:T(512)S(1)} %bitcast.31, bf16[512,1024]{1,0:T(8,128)(2,1)S(1)} %multiply_convert_fusion), kind=kCustom, calls=%fused_computation.1 | custom fusion | bytes 3149824 | tf_op jit(solution)/shard_map/scatter | solution.py:29
  116.0 0.0 all-to-all-done
  116.0 9.8 %all-to-all-start.1 = ((bf16[128,8,1024]{2,1,0:T(8,128)(2,1)}), bf16[128,8,1024]{2,1,0:T(8,128)(2,1)S(1)}, u32[]{:S(2)}, u32[]{:S(2)}) async-start(bf16[128,8,1024]{2,1,0:T(8,128)(2,1)} %scatter_fusion.1), calls=%async_computation.1 | async-start | bytes 4194304 | tf_op jit(solution)/shard_map/all_to_all | solution.py:32
  125.9 0.0 all-gather.3.cloned.1.call-start
  125.9 0.5 broadcast.155
  126.4 0.8 reduce.3
  127.2 0.1 reshape.97
  127.3 28.0 %all-to-all-done.1 = bf16[128,8,1024]{2,1,0:T(8,128)(2,1)S(1)} async-done(((bf16[128,8,1024]{2,1,0:T(8,128)(2,1)}), bf16[128,8,1024]{2,1,0:T(8,128)(2,1)S(1)}, u32[]{:S(2)}, u32[]{:S(2)}) %all-to-all-start.1) | async-done | bytes 2097184 | tf_op jit(solution)/shard_map/all_to_all | solution.py:32
  155.4 0.0 copy-start.1
  155.4 6.2 %scatter_custom_fusion.2 = bf16[512,1024]{1,0:T(8,128)(2,1)} fusion(s32[1024]{0:T(1024)S(1)} %bitcast.40, bf16[128,8,1024]{2,1,0:T(8,128)(2,1)S(1)} %all-to-all-done.1, bf16[]{:T(256)} %constant.48.clone.1), kind=kCustom, calls=%fused_computation.6 | custom fusion | bytes 3145730 | tf_op jit(solution)/shard_map/scatter | solution.py:38
  161.6 0.0 all-gather.3.cloned.1.call-update
  161.6 0.0 copy-done.1
  161.6 18.2 %all-gather = s32[1,8192]{1,0:T(1,128)S(1)} all-gather(s32[1,512]{1,0:T(1,128)S(1)} %copy-done.1), channel_id=2, replica_groups=mesh['row'=8,'col'=16] {'col'}, dimensions={1}, use_global_device_ids=true | all-gather | bytes 34816 | tf_op jit(solution)/shard_map/all_gather | solution.py:46
  179.9 90.1 %all-gather.3.cloned.1.call-done = bf16[8192,1024]{1,0:T(8,128)(2,1)} async-done(((bf16[512,1024]{1,0:T(8,128)(2,1)}), bf16[8192,1024]{1,0:T(8,128)(2,1)}) %all-gather.3.cloned.1.call-update) | async-done | bytes 16777232 | tf_op jit(solution)/shard_map/all_gather | solution.py:45
  269.9 14.1 %select_reduce_fusion = f32[512]{0:T(512)S(1)} fusion(bf16[512,1024]{1,0:T(8,128)(2,1)} %scatter_custom_fusion.2, bf16[8192,1024]{1,0:T(8,128)(2,1)} %all-gather.3.cloned.1.call-done, s32[512]{0:T(512)S(1)} %iota_add_fusion, s32[8192]{0:T(1024)S(1)} %bitcast.34, s32[512]{0:T(512)S(1)} %bitcast.41), kind=kOutput, calls=%fused_computation.3 | convolution fusion | flops 8610906112 | bytes 17864704 | tf_op jit(solution)/shard_map/dot_general | solution.py:13
  284.1 0.6 broadcast_maximum_fusion
  (12 shorter events, 0.1 us)
Async XLA Ops:
  7.9 34.2 %copy-start = (f32[512,1024]{1,0:T(8,128)S(1)}, f32[512,1024]{1,0:T(8,128)}, u32[]{:S(2)}) copy-start(f32[512,1024]{1,0:T(8,128)} %param.3) | copy-start | bytes 6291460
  30.7 85.3 %all-to-all-start = ((s32[128,1,8]{2,1,0:T(1,128)}), s32[128,1,8]{2,1,0:T(1,128)S(1)}, u32[]{:S(2)}, u32[]{:S(2)}) async-start(s32[128,1,8]{2,1,0:T(1,128)} %copy.9), calls=%async_computation | async-start | bytes 131072 | tf_op jit(solution)/shard_map/all_to_all | solution.py:33
  116.0 39.4 %all-to-all-start.1 = ((bf16[128,8,1024]{2,1,0:T(8,128)(2,1)}), bf16[128,8,1024]{2,1,0:T(8,128)(2,1)S(1)}, u32[]{:S(2)}, u32[]{:S(2)}) async-start(bf16[128,8,1024]{2,1,0:T(8,128)(2,1)} %scatter_fusion.1), calls=%async_computation.1 | async-start | bytes 4194304 | tf_op jit(solution)/shard_map/all_to_all | solution.py:32
  125.9 144.1 %all-gather.3.cloned.1.call-start = ((), (), s32[]{:S(2)}) async-start(), calls=%async_computation.2 | async-start | bytes 17825792 | tf_op jit(solution)/shard_map/all_gather | solution.py:45
  155.4 6.3 %copy-start.1 = (s32[1,512]{1,0:T(1,128)S(1)}, s32[1,512]{1,0:T(1,128)}, u32[]{:S(2)}) copy-start(s32[1,512]{1,0:T(1,128)} %param.5) | copy-start | bytes 6148
Sparse Core Ops, SparseCore 0:
  161.7 108.1 all-gather.2
where the time goes:
time: 295 us; the launch traced here: 291 us
  waiting for transfers between devices  118 us (40%)
  local copies, waits for them, and re-layouts  103 us (35%)
  starting transfers between devices  21.4 us (7%)
  blocking collectives  18.2 us (6%)
  matrix products  14.1 us (5%)
  between operations  13.5 us (5%)
  other arithmetic  3.01 us (1%)
    all_gather x1, waiting for transfers between devices, shards(): other = lax.all_gather(mine, 'col', axis=0, tiled=True)  90.1 us
    scatter x1, local copies, waits for them, and re-layouts, shards(): jnp.zeros((devs, slots, width), jnp.bfloat16).at[target, slot].set(unit)  71.8 us
    all_to_all x1, waiting for transfers between devices, shards(): lax.all_to_all(send_rows, ('row', 'col'), split_axis=0, concat_axis=0, ti...  28 us
    scatter x1, local copies, waits for them, and re-layouts, shards(): jnp.full((devs, slots), rows_dev, jnp.int32).at[target, slot].set(place)  22 us
    all_gather x1, blocking collectives, shards(): other_labels = lax.all_gather(labels, 'col', axis=0, tiled=True)  18.2 us
    dot_general x1, matrix products, masked_sims(): lax.dot_general(left, right, (((1,), (1,)), ((), ())), preferred_element_...  14.1 us
    all_to_all x1, starting transfers between devices, shards(): lax.all_to_all(send_places, ('row', 'col'), split_axis=0, concat_axis=0,...  11.5 us
    all_to_all x1, starting transfers between devices, shards(): lax.all_to_all(send_rows, ('row', 'col'), split_axis=0, concat_axis=0, ti...  9.85 us
  transfers between devices with their start and end apart: 3, of which 2 were waited for; matrix products, arithmetic and copies ran while one was open for 26% of the time, Pallas kernels for 0%

commit v1 on v0

v1 whole, which is shorter than its diff:
```python
import functools

import jax
import jax.numpy as jnp
from jax import lax
from jax.experimental import pallas as pl
from jax.experimental.pallas import tpu as pltpu
from jax.sharding import PartitionSpec as P

MESH = pl.DeviceIdType.MESH
F32, BF16, I32 = jnp.float32, jnp.bfloat16, jnp.int32
DEVS = 128
ROWS = 512
WIDTH = 1024
HALF = WIDTH // 2
QUARTER = ROWS // 2
CHIP = (0, 1, 7, 2, 5, 4, 6, 3)
VERTEX = (0, 1, 3, 7, 5, 4, 6, 2)
HELD = ((0, 1, 9, 4), (1, 0, 2, 3), (8, 2, 0, 6), (2, 8, 1, 7), (5, 4, 6, 1), (4, 5, 3, 2), (6, 3, 5, 9), (3, 7, 4, 8))
SLOT = (0, 512, 1024, 1536)
SECOND, PATCH, HEAD = 2048, 2560, 2816
HEAD_ROWS = 272
X_ROWS = HEAD + HEAD_ROWS
SEND = (
    (0, 0, 0, 0, 0, 0, SECOND, 0),
    (0, 0, SECOND, 0, 0, 0, 0, 0),
    (512, 1024, SECOND, 512, 512, 1024, 0, 512),
)
PATCH_BLOCK = (5, 5, 5, 0, 0, 0, 0, 5)
PATCH_HALF = (0, 1, 0, 0, 0, 0, 1, 1)
PATCH_MEETS = (0, 512, 0, 1536, 0, 0, SECOND, 1536)
CHUNKS = 4
CHUNK = ROWS // CHUNKS


def pick(p, table):
    out = jnp.int32(table[0])
    for i in range(1, len(table)):
        if table[i] != table[0]:
            out = jnp.where(p == i, jnp.int32(table[i]), out)
    return out


def iota(shape, dim):
    return lax.broadcasted_iota(I32, shape, dim)


def ones(cond):
    return jnp.where(cond, jnp.float32(1.0), jnp.float32(0.0)).astype(BF16)


def dot_t(a, b):
    return lax.dot_general(a, b, (((1,), (1,)), ((), ())), preferred_element_type=F32)


def dot(a, b):
    return lax.dot_general(a, b, (((1,), (0,)), ((), ())), preferred_element_type=F32)


def kernel(
    emb_ref, dest_ref, ids_ref, out_ref,
    emb, unit, sbuf, rb, meta_s, meta_r, labs, q, xs, acc, ob, fin,
    emb_sem, own_sem, row_s, row_r, meta_ss, meta_rr, lab_s, lab_r,
    ici_s, ici_r, pair_s, pair_r, patch_s, patch_r, head_s, head_r, fin_s, fin_r,
):
    row, col = lax.axis_index("row"), lax.axis_index("col")
    x, k, y, z = row // 2, row % 2, col // 4, col % 4
    chip = x * 16 + y * 4 + z
    me = chip * 2 + k
    gx, gy, gz = x // 2, y // 2, z // 2
    group = (1 - gx) * 4 + gy * 2 + gz
    p = (x % 2) * 4 + (y % 2) * 2 + z % 2
    share = pick(p, CHIP)
    large_only = (p == 2) | (p == 6)

    emb_copy = pltpu.make_async_copy(emb_ref, emb, emb_sem)
    emb_copy.start()

    def relative(e):
        off = (e * 45) % DEVS
        dx, dy, dz, dk = off // 32, (off // 8) % 4, (off // 2) % 4, off % 2
        return (x + dx) % 4, (y + dy) % 4, (z + dz) % 4, (k + dk) % 2

    barrier = pltpu.get_barrier_semaphore()

    def greet(e, _):
        tx, ty, tz, tk = relative(e)
        pl.semaphore_signal(barrier, inc=1, device_id=(2 * tx + tk, 4 * ty + tz), device_id_type=MESH)
        return _

    lax.fori_loop(1, DEVS, greet, 0)

    dest = dest_ref[...]
    block = lax.shift_right_logical(dest, 9)
    place = dest & 511
    g, b = lax.shift_right_logical(block, 4), block & 15
    to = jnp.where(b < 6, b, jnp.where(b < 8, 6, jnp.where(b < 10, 7, b - 10)))
    half = jnp.where(b < 6, 0, jnp.where(b < 10, b & 1, 1))
    vert = pick(to, VERTEX)
    tx = 2 * (1 - lax.shift_right_logical(g, 2)) + lax.shift_right_logical(vert, 2)
    ty = 2 * (lax.shift_right_logical(g, 1) & 1) + (lax.shift_right_logical(vert, 1) & 1)
    tz = 2 * (g & 1) + (vert & 1)
    tchip = tx * 16 + ty * 4 + tz
    tb = tchip * 2 + half
    hot = iota((DEVS, ROWS), 0) == tb
    before = ones(iota((ROWS, ROWS), 0) < iota((ROWS, ROWS), 1))
    rank = dot(ones(hot), before)
    slot = jnp.sum(jnp.where(hot, rank, 0.0), axis=0, keepdims=True).astype(I32)
    line = tb * 8 + slot

    value = place + 1 + 512 * half
    to_chip = iota((64, ROWS), 0) == tchip
    lanes = ones(iota((128, ROWS), 0) == (half * 8 + slot + 16 * (me % 8)))
    high = jnp.where(to_chip, lax.shift_right_logical(value, 4).astype(F32), 0.0).astype(BF16)
    low = jnp.where(to_chip, (value & 15).astype(F32), 0.0).astype(BF16)
    meta = 16.0 * dot_t(high, lanes) + dot_t(low, lanes)
    for n in range(64):
        meta_s[n] = meta[n : n + 1, :]

    emb_copy.wait()
    rows = emb[...]
    scale = lax.rsqrt(jnp.sum(rows * rows, axis=1, keepdims=True) + 1e-06)
    unit[...] = (rows * scale).astype(BF16)
    for a in range(8):
        take = ones(iota((128, ROWS), 0) + 128 * a == line)
        packed = dot(take, unit[...]).astype(BF16)
        sbuf[0, pl.ds(128 * a, 128), :] = packed[:, :HALF]
        sbuf[1, pl.ds(128 * a, 128), :] = packed[:, HALF:]

    pl.semaphore_wait(barrier, DEVS - 1)

    def send_rows(e, _):
        tx, ty, tz, tk = relative(e)
        n = tx * 16 + ty * 4 + tz
        pltpu.make_async_remote_copy(
            src_ref=sbuf.at[tk, pl.ds(pl.multiple_of(16 * n, 16), 16)],
            dst_ref=rb.at[pl.ds(pl.multiple_of(16 * me, 16), 16)],
            send_sem=row_s, recv_sem=row_r,
            device_id=(2 * tx + tk, 4 * ty + tz), device_id_type=MESH,
        ).start()
        return _

    def send_meta(e, _):
        tx, ty, tz, tk = relative(e)
        n = tx * 16 + ty * 4 + tz
        pltpu.make_async_remote_copy(
            src_ref=meta_s.at[n], dst_ref=meta_r.at[me],
            send_sem=meta_ss, recv_sem=meta_rr,
            device_id=(2 * tx + tk, 4 * ty + tz), device_id_type=MESH,
        ).start()
        return _

    def send_ids(j, _):
        v, tk = j // 2, j % 2
        hx = 2 * (1 - row // 4) + v // 4
        hy = 2 * ((row // 2) % 2) + (v // 2) % 2
        hz = 2 * (row % 2) + v % 2
        pltpu.make_async_remote_copy(
            src_ref=ids_ref, dst_ref=labs.at[col],
            send_sem=lab_s, recv_sem=lab_r,
            device_id=(2 * hx + tk, 4 * hy + hz), device_id_type=MESH,
        ).start()
        return _

    lax.fori_loop(1, 17, send_rows, 0)
    lax.fori_loop(0, 16, send_ids, 0)
    lax.fori_loop(1, DEVS, send_meta, 0)
    lax.fori_loop(17, DEVS, send_rows, 0)
    own_copy = pltpu.make_async_copy(
        sbuf.at[k, pl.ds(pl.multiple_of(16 * chip, 16), 16)],
        rb.at[pl.ds(pl.multiple_of(16 * me, 16), 16)], own_sem,
    )
    own_copy.start()
    meta_r[me] = meta_s[chip]

    pltpu.make_async_copy(labs, labs, lab_r).wait()
    large = labs[7, :, 0:1]
    first = jnp.where(share < 6, share, 2 * share - 6)
    second = jnp.where(share < 6, share + 10, 2 * share - 5)
    is_large = labs[first] == large
    eye = ones(iota((ROWS, ROWS), 0) == iota((ROWS, ROWS), 1))

    def column(r):
        return dot_t(eye, jnp.broadcast_to(r, (8, ROWS)).astype(BF16))[:, 0:1]

    rest_ids = jnp.where(is_large, labs[second], labs[first]).astype(F32)
    rest_col = column(rest_ids)
    large_col = column(jnp.where(is_large, 1.0, 0.0))
    index_col = iota((ROWS, 1), 0).astype(F32) + 1.0
    key_large = index_col + 512.0 * (1.0 - large_col)
    key_rest = index_col + 512.0 * large_col

    pltpu.make_async_copy(meta_r.at[pl.ds(0, DEVS - 1)], meta_r.at[pl.ds(0, DEVS - 1)], meta_rr).wait()
    for a in range(16):
        r = meta_r[8 * a]
        for i in range(1, 8):
            r = r + meta_r[8 * a + i]
        q[0:ROWS, pl.ds(128 * a, 128)] = ones(key_large == r)
        q[ROWS : 2 * ROWS, pl.ds(128 * a, 128)] = ones(key_rest == r)

    own_copy.wait()
    pltpu.make_async_copy(rb.at[pl.ds(0, 16 * (DEVS - 1))], rb.at[pl.ds(0, 16 * (DEVS - 1))], row_r).wait()
    xs[k, pl.ds(0, ROWS), :] = dot(q[0:ROWS, :], rb[...]).astype(BF16)
    xs[k, pl.ds(SECOND, ROWS), :] = dot(q[ROWS : 2 * ROWS, :], rb[...]).astype(BF16)

    def along(bit):
        nx = x + 1 - 2 * (x % 2) if bit == 2 else x
        ny = y + 1 - 2 * (y % 2) if bit == 1 else y
        nz = z + 1 - 2 * (z % 2) if bit == 0 else z
        return (2 * nx + k, 4 * ny + nz)

    def between(src, dst, n, send, recv, device):
        return pltpu.make_async_remote_copy(
            src_ref=xs.at[k, pl.ds(src, n)], dst_ref=xs.at[k, pl.ds(dst, n)],
            send_sem=send, recv_sem=recv, device_id=device, device_id_type=MESH,
        )

    sibling = (2 * x + 1 - k, col)
    pairs = []

    def share_rows(start, n):
        i = len(pairs)
        cp = between(start, start, n, pair_s.at[i], pair_r.at[i], sibling)
        cp.start()
        pairs.append(cp)

    def block_copy(bit, c):
        src = pl.multiple_of(pick(p, SEND[bit]) + CHUNK * c, 16)
        return between(src, SLOT[1 + bit] + CHUNK * c, CHUNK, ici_s.at[bit, c], ici_r.at[bit, c], along(bit))

    copies = [[block_copy(bit, c) for c in range(CHUNKS)] for bit in range(3)]
    for c in range(CHUNKS):
        copies[0][c].start()
        copies[1][c].start()

        @pl.when(large_only)
        def _():
            copies[2][c].start()

    def patch_copy(i, src, bit):
        return between(src, PATCH, QUARTER, patch_s.at[i], patch_r, along(bit))

    @pl.when(p == 4)
    def _():
        patch_copy(0, 0, 2).start()

    head_steps = ((1, 0), (3, 1), (7, 2), (5, 1), (4, 0))
    for v, bit in head_steps:
        @pl.when(p == v)
        def _():
            between(SECOND, HEAD, HEAD_ROWS, head_s, head_r, along(bit)).start()

    share_rows(0, ROWS)
    share_rows(SECOND, ROWS)
    for c in range(CHUNKS):
        for bit in range(2):
            copies[bit][c].wait_recv()
            share_rows(SLOT[1 + bit] + CHUNK * c, CHUNK)

        @pl.when(jnp.logical_not(large_only))
        def _():
            copies[2][c].start()

    @pl.when(p == 5)
    def _():
        patch_copy(0, 768, 2).start()

    @pl.when(p == 2)
    def _():
        patch_copy(0, 1024, 0).start()
        patch_copy(1, 1280, 2).start()

    @pl.when(p == 6)
    def _():
        patch_copy(0, 1024, 2).start()
        patch_copy(1, 1280, 0).start()

    for c in range(CHUNKS):
        copies[2][c].wait_recv()
        share_rows(SLOT[3] + CHUNK * c, CHUNK)

    has_patch = (p != 4) & (p != 5)
    has_head = (p != 2) & (p != 6) & (p != 4)
    n_pairs = len(pairs)
    patch_pair = between(PATCH, PATCH, QUARTER, pair_s.at[n_pairs], pair_r.at[n_pairs], sibling)
    head_pair = between(HEAD, HEAD, HEAD_ROWS, pair_s.at[n_pairs + 1], pair_r.at[n_pairs + 1], sibling)

    @pl.when(has_head)
    def _():
        pltpu.make_async_copy(xs.at[k, pl.ds(HEAD, HEAD_ROWS)], xs.at[k, pl.ds(HEAD, HEAD_ROWS)], head_r).wait()
        head_pair.start()

    @pl.when(has_patch)
    def _():
        pltpu.make_async_copy(xs.at[k, pl.ds(PATCH, QUARTER)], xs.at[k, pl.ds(PATCH, QUARTER)], patch_r).wait()
        patch_pair.start()

    for cp in pairs:
        cp.wait_recv()

    @pl.when(has_head)
    def _():
        head_pair.wait_recv()

    @pl.when(has_patch)
    def _():
        patch_pair.wait_recv()

    def tile(j, nj, i, ni):
        return dot_t(xs[0, pl.ds(j, nj), :], xs[0, pl.ds(i, ni), :]) + dot_t(
            xs[1, pl.ds(j, nj), :], xs[1, pl.ds(i, ni), :]
        )

    def top(t):
        return jnp.max(t, axis=0, keepdims=True)

    mine = pl.multiple_of(QUARTER * k, QUARTER)
    own_tile = iota((ROWS, QUARTER), 0) == iota((ROWS, QUARTER), 1) + QUARTER * k
    ob[...] = jnp.full(ob.shape, -1.0, F32)
    for s in range(4):
        best = None
        for j in range(4):
            t = tile(SLOT[j], ROWS, pl.multiple_of(SLOT[s] + mine, QUARTER), QUARTER)
            if s == j:
                t = jnp.where(own_tile, -1.0, t)
            m = top(t)
            best = m if best is None else jnp.maximum(best, m)
        acc[s] = best
    rest_row = jnp.where(k == 0, rest_ids[:, :QUARTER], rest_ids[:, QUARTER:])
    second_cols = pl.multiple_of(SECOND + mine, QUARTER)
    t = tile(SECOND, ROWS, second_cols, QUARTER)
    acc[4] = top(jnp.where((rest_col == rest_row) & jnp.logical_not(own_tile), t, -1.0))

    def raise_to(b, at, n, v):
        ob[b, :, pl.ds(at, n)] = jnp.maximum(ob[b, :, pl.ds(at, n)], v)

    @pl.when(large_only)
    def _():
        for s in range(4):
            t = tile(SECOND, ROWS, pl.multiple_of(SLOT[s] + mine, QUARTER), QUARTER)
            acc[s] = jnp.maximum(acc[s], top(t))
            acc[4] = jnp.maximum(acc[4], top(tile(SLOT[s], ROWS, second_cols, QUARTER)))

    @pl.when(has_head)
    def _():
        nxt = labs[share + 1]
        head_ids = jnp.where(nxt == large, labs[share + 11], nxt).astype(F32)
        head_col = column(head_ids)[:HEAD_ROWS]
        t = tile(HEAD, HEAD_ROWS, second_cols, QUARTER)
        acc[4] = jnp.maximum(acc[4], top(jnp.where(head_col == rest_row, t, -1.0)))
        t = tile(second_cols, QUARTER, HEAD, HEAD_ROWS)
        some_col = jnp.where(k == 0, rest_col[:QUARTER], rest_col[QUARTER:])
        m = top(jnp.where(some_col == head_ids[:, :HEAD_ROWS], t, -1.0))
        m = jnp.concatenate([m, jnp.full((1, ROWS - HEAD_ROWS), -1.0, F32)], axis=1)
        raise_to(share + 1, 0, ROWS, jnp.where(nxt == large, -1.0, m))
        raise_to(share + 11, 0, ROWS, jnp.where(nxt == large, m, -1.0))

    @pl.when(has_patch)
    def _():
        meets = pick(p, PATCH_MEETS)
        t = tile(PATCH, QUARTER, pl.multiple_of(meets + mine, QUARTER), QUARTER)
        s = jnp.where(meets == SECOND, 4, meets // ROWS)
        acc[s] = jnp.maximum(acc[s], top(t))
        t = tile(pl.multiple_of(meets, ROWS), ROWS, pl.multiple_of(PATCH + 128 * k, 128), 128)
        at = pl.multiple_of(QUARTER * pick(p, PATCH_HALF) + 128 * k, 128)
        v = pick(p, PATCH_BLOCK)
        here = labs[v, :, pl.ds(at, 128)] == large
        raise_to(v, at, 128, jnp.where(here, top(t), -1.0))
        raise_to(v + 10, at, 128, jnp.where(here, -1.0, top(t)))

    for s in range(4):
        v = pick(p, tuple(h[s] for h in HELD))
        here = labs[v, :, pl.ds(mine, QUARTER)] == large
        raise_to(v, mine, QUARTER, jnp.where(here, acc[s], -1.0))

        @pl.when(v < 6)
        def _():
            raise_to(v + 10, mine, QUARTER, jnp.where(here, -1.0, acc[s]))

    here = labs[first, :, pl.ds(mine, QUARTER)] == large
    raise_to(second, mine, QUARTER, jnp.where(here, acc[4], -1.0))
    raise_to(first, mine, QUARTER, jnp.where(here, -1.0, acc[4]))

    def send_best(b, _):
        pltpu.make_async_remote_copy(
            src_ref=ob.at[b], dst_ref=fin.at[p * 2 + k],
            send_sem=fin_s, recv_sem=fin_r, device_id=(group, b), device_id_type=MESH,
        ).start()
        return _

    lax.fori_loop(0, 16, send_best, 0)

    pltpu.make_async_copy(sbuf.at[0, pl.ds(0, 1008)], sbuf.at[0, pl.ds(0, 1008)], row_s).wait()
    pltpu.make_async_copy(sbuf.at[0], sbuf.at[0], row_s).wait()
    pltpu.make_async_copy(meta_r.at[pl.ds(0, DEVS - 1)], meta_r.at[pl.ds(0, DEVS - 1)], meta_ss).wait()
    pltpu.make_async_copy(labs, labs, lab_s).wait()
    for per_bit in copies:
        for cp in per_bit:
            cp.wait_send()
    for cp in pairs:
        cp.wait_send()

    @pl.when(has_head)
    def _():
        head_pair.wait_send()

    @pl.when(has_patch)
    def _():
        patch_pair.wait_send()

    @pl.when((p == 1) | (p == 3) | (p == 7) | (p == 5) | (p == 4))
    def _():
        between(SECOND, HEAD, HEAD_ROWS, head_s, head_r, along(0)).wait_send()

    @pl.when((p == 4) | (p == 5) | (p == 2) | (p == 6))
    def _():
        patch_copy(0, 0, 0).wait_send()

    @pl.when((p == 2) | (p == 6))
    def _():
        patch_copy(1, 0, 0).wait_send()

    pltpu.make_async_copy(fin, fin, fin_s).wait()
    pltpu.make_async_copy(fin, fin, fin_r).wait()
    best = fin[0]
    for i in range(1, 16):
        best = jnp.maximum(best, fin[i])
    out_ref[...] = best


def shards(embeddings, dest_pos, cluster_ids):
    dma, n_pairs = pltpu.SemaphoreType.DMA, 4 + 3 * CHUNKS
    return pl.pallas_call(
        kernel,
        out_shape=jax.ShapeDtypeStruct((1, ROWS), F32),
        in_specs=[
            pl.BlockSpec(memory_space=pl.ANY),
            pl.BlockSpec(memory_space=pltpu.VMEM),
            pl.BlockSpec(memory_space=pltpu.VMEM),
        ],
        out_specs=pl.BlockSpec(memory_space=pltpu.VMEM),
        scratch_shapes=[
            pltpu.VMEM((ROWS, WIDTH), F32),
            pltpu.VMEM((ROWS, WIDTH), BF16),
            pltpu.VMEM((2, 1024, HALF), BF16),
            pltpu.VMEM((16 * DEVS, HALF), BF16),
            pltpu.VMEM((64, 1, 128), F32),
            pltpu.VMEM((DEVS, 1, 128), F32),
            pltpu.VMEM((16, 1, ROWS), I32),
            pltpu.VMEM((2 * ROWS, 16 * DEVS), BF16),
            pltpu.VMEM((2, X_ROWS, HALF), BF16),
            pltpu.VMEM((5, 1, QUARTER), F32),
            pltpu.VMEM((16, 1, ROWS), F32),
            pltpu.VMEM((16, 1, ROWS), F32),
            dma, dma, dma, dma, dma, dma, dma, dma,
            dma((3, CHUNKS)), dma((3, CHUNKS)), dma((n_pairs,)), dma((n_pairs,)),
            dma((2,)), dma, dma, dma, dma, dma,
        ],
        compiler_params=pltpu.CompilerParams(
            collective_id=0, has_side_effects=True, vmem_limit_bytes=44 * 2**20
        ),
        name="best_match",
    )(embeddings, dest_pos.reshape(1, ROWS), cluster_ids)


def solution(mesh):
    return jax.shard_map(
        shards,
        mesh=mesh,
        in_specs=(P(("row", "col"), None), P(("row", "col")), P("row", "col")),
        out_specs=P("row", "col"),
        check_vma=False,
    )
```

time: 295 us -> 86.9 us (0.29); the launches traced: 291 us -> 86.7 us
  waiting for transfers between devices: 118 us -> 0 us
  local copies, waits for them, and re-layouts: 103 us -> 3.53 us
  Pallas kernels: 0 us -> 83.1 us
  starting transfers between devices: 21.4 us -> 0 us
  blocking collectives: 18.2 us -> 0 us
  matrix products: 14.1 us -> 0 us
  between operations: 13.5 us -> 0.01 us
  other arithmetic: 3.01 us -> 0 us
    scatter x3 -> x0, local copies, waits for them, and re-layouts: 100 us -> none  [the longest x1 71.8 us: shards(): jnp.zeros((devs, slots, width), jnp.bfloat16).at[target, slot].set(unit)]
    all_gather x1 -> x0, waiting for transfers between devices: 90.1 us -> none  [shards(): other = lax.all_gather(mine, 'col', axis=0, tiled=True)]
    pallas_call x0 -> x1, Pallas kernels: none -> 83.1 us  [shards(): pl.pallas_call(kernel, out_shape=jax.ShapeDtypeStruct((1, ROWS), F32), in...]
    all_to_all x2 -> x0, waiting for transfers between devices: 28 us -> none  [the longest x1 28 us: shards(): lax.all_to_all(send_rows, ('row', 'col'), split_axis=0, concat_axis=0, ti...]
    all_to_all x2 -> x0, starting transfers between devices: 21.3 us -> none  [the longest x1 11.5 us: shards(): lax.all_to_all(send_places, ('row', 'col'), split_axis=0, concat_axis=0,...]
    all_gather x1 -> x0, blocking collectives: 18.2 us -> none  [shards(): other_labels = lax.all_gather(labels, 'col', axis=0, tiled=True)]
    dot_general x1 -> x0, matrix products: 14.1 us -> none  [masked_sims(): lax.dot_general(left, right, (((1,), (1,)), ((), ())), preferred_element_...]
    unnamed x5 -> x7, local copies, waits for them, and re-layouts: 0.02 us -> 3.53 us
  transfers between devices with their start and end apart: 3 -> 0, of which waited for: 2 -> 0; matrix products, arithmetic and copies ran while one was open for 26% -> 0% of each run, Pallas kernels for 0% -> 0%
where the time goes in v1:
time: 86.9 us; the launch traced here: 86.7 us
  Pallas kernels  83.1 us (96%)
  local copies, waits for them, and re-layouts  3.53 us (4%)
    pallas_call x1, Pallas kernels, shards(): pl.pallas_call(kernel, out_shape=jax.ShapeDtypeStruct((1, ROWS), F32), in...  83.1 us
    unnamed x7, local copies, waits for them, and re-layouts  3.53 us

profile of v1, /device:TPU:1, one launch (start us, length us, event | category | flops | bytes accessed | tf_op | source)
XLA Modules:
  0.0 86.7 jit_solution(5890710935685048565)
XLA Ops:
  0.0 0.0 copy-start
  0.0 1.6 %copy-done = f32[512,1024]{1,0:T(8,128)S(1)} copy-done((f32[512,1024]{1,0:T(8,128)S(1)}, f32[512,1024]{1,0:T(8,128)}, u32[]{:S(2)}) %copy-start) | copy-done | bytes 2097176
  1.6 0.0 copy-start.1
  1.6 0.7 copy-done.1
  2.3 0.0 copy-start.2
  2.3 0.7 copy-done.2
  3.0 83.1 %best_match.1 = f32[1,512]{1,0:T(1,128)S(1)} custom-call(f32[512,1024]{1,0:T(8,128)S(1)} %copy-done, s32[1,512]{1,0:T(1,128)S(1)} %bitcast.1, s32[1,512]{1,0:T(1,128)S(1)} %copy-done.2), custom_call_target="tpu_custom_call" | custom-call | tf_op jit(solution)/shard_map/best_match/pallas_call | solution.py:433
  86.1 0.6 copy.5
Async XLA Ops:
  0.0 1.6 %copy-start = (f32[512,1024]{1,0:T(8,128)S(1)}, f32[512,1024]{1,0:T(8,128)}, u32[]{:S(2)}) copy-start(f32[512,1024]{1,0:T(8,128)} %emb_ref.1) | copy-start | bytes 6291460
  1.6 0.7 copy-start.1
  2.3 0.7 copy-start.2

commit v2 on v1

v2 whole, which is shorter than its diff:
```python
import functools

import jax
import jax.numpy as jnp
from jax import lax
from jax.experimental import pallas as pl
from jax.experimental.pallas import tpu as pltpu
from jax.sharding import PartitionSpec as P

MESH = pl.DeviceIdType.MESH
F32, BF16, I32 = jnp.float32, jnp.bfloat16, jnp.int32
DEVS = 128
ROWS = 512
WIDTH = 1024
HALF = WIDTH // 2
QUARTER = ROWS // 2
CHIP = (0, 1, 7, 2, 5, 4, 6, 3)
VERTEX = (0, 1, 3, 7, 5, 4, 6, 2)
HELD = ((0, 1, 9, 4), (1, 0, 2, 3), (8, 2, 0, 6), (2, 8, 1, 7), (5, 4, 6, 1), (4, 5, 3, 2), (6, 3, 5, 9), (3, 7, 4, 8))
SLOT = (0, 512, 1024, 1536)
SECOND, PATCH, HEAD = 2048, 2560, 2816
HEAD_ROWS = 272
X_ROWS = HEAD + HEAD_ROWS
SEND = (
    (0, 0, 0, 0, 0, 0, SECOND, 0),
    (0, 0, SECOND, 0, 0, 0, 0, 0),
    (512, 1024, SECOND, 512, 512, 1024, 0, 512),
)
PATCH_BLOCK = (5, 0, 5, 0, 0, 0, 0, 5)
PATCH_HALF = (1, 0, 0, 0, 0, 0, 1, 1)
PATCH_MEETS = (0, 0, 0, 1536, 0, 0, SECOND, 1536)
PATCHES = ((4, 0, 2, 256), (6, 2, 2, 1024), (6, 7, 0, 1280), (2, 3, 0, 1024), (2, 6, 2, 1280))
CHUNKS = ((0, 64), (64, 64), (128, 128), (256, 128), (384, 128))


def pick(p, table):
    out = jnp.int32(table[0])
    for i in range(1, len(table)):
        if table[i] != table[0]:
            out = jnp.where(p == i, jnp.int32(table[i]), out)
    return out


def iota(shape, dim):
    return lax.broadcasted_iota(I32, shape, dim)


def ones(cond):
    return jnp.where(cond, jnp.float32(1.0), jnp.float32(0.0)).astype(BF16)


def dot_t(a, b):
    return lax.dot_general(a, b, (((1,), (1,)), ((), ())), preferred_element_type=F32)


def dot(a, b):
    return lax.dot_general(a, b, (((1,), (0,)), ((), ())), preferred_element_type=F32)


def kernel(
    emb_hbm, dest_hbm, ids_hbm, out_ref,
    emb, dest_ref, ids_ref, unit, sbuf, rb, meta_s, meta_r, labs, q, xs, acc, ob, fin,
    emb_sem, dest_sem, ids_sem, own_sem, row_s, row_r, meta_ss, meta_rr, lab_s, lab_r,
    ici_s, ici_r, pair_s, pair_r, patch_s, patch_r, head_s, head_r, fin_s, fin_r,
):
    row, col = lax.axis_index("row"), lax.axis_index("col")
    x, k, y, z = row // 2, row % 2, col // 4, col % 4
    chip = x * 16 + y * 4 + z
    me = chip * 2 + k
    group = 2 * x + y // 2
    p = (y % 2) * 4 + (z // 2) * 2 + (z // 2 + z) % 2
    share = pick(p, CHIP)
    large_only = (p == 2) | (p == 6)

    dest_copy = pltpu.make_async_copy(dest_hbm, dest_ref, dest_sem)
    dest_copy.start()
    emb_copy = pltpu.make_async_copy(emb_hbm, emb, emb_sem)
    emb_copy.start()
    ids_copy = pltpu.make_async_copy(ids_hbm, ids_ref, ids_sem)
    ids_copy.start()

    def relative(e):
        off = (e * 45) % DEVS
        dx, dy, dz, dk = off // 32, (off // 8) % 4, (off // 2) % 4, off % 2
        return (x + dx) % 4, (y + dy) % 4, (z + dz) % 4, (k + dk) % 2

    barrier = pltpu.get_barrier_semaphore()

    def greet(tx, ty, tz, tk):
        pl.semaphore_signal(barrier, inc=1, device_id=(2 * tx + tk, 4 * ty + tz), device_id_type=MESH)

    lead = (x % 2 == 0) & (y % 2 == 0) & (z % 2 == 1) & (k == 0)
    root = (x == 2) & (y == 2) & (z == 3) & (k == 0)

    @pl.when(jnp.logical_not(lead))
    def _():
        greet(x - x % 2, y - y % 2, z - z % 2 + 1, 0)

    dest_copy.wait()
    dest = dest_ref[...]
    block = lax.shift_right_logical(dest, 9)
    place = dest & 511
    g, b = lax.shift_right_logical(block, 4), block & 15
    to = jnp.where(b < 6, b, jnp.where(b < 8, 6, jnp.where(b < 10, 7, b - 10)))
    half = jnp.where(b < 6, 0, jnp.where(b < 10, b & 1, 1))
    vert = pick(to, VERTEX)
    tx = lax.shift_right_logical(g, 1)
    ty = 2 * (g & 1) + lax.shift_right_logical(vert, 2)
    tz = (vert & 2) + (lax.shift_right_logical(vert, 1) + vert & 1)
    tchip = tx * 16 + ty * 4 + tz
    tb = tchip * 2 + half
    hot = iota((DEVS, ROWS), 0) == tb
    before = ones(iota((ROWS, ROWS), 0) < iota((ROWS, ROWS), 1))
    rank = dot(ones(hot), before)
    slot = jnp.sum(jnp.where(hot, rank, 0.0), axis=0, keepdims=True).astype(I32)
    line = tb * 8 + slot

    value = place + 1 + 512 * half
    to_chip = iota((64, ROWS), 0) == tchip
    lanes = ones(iota((128, ROWS), 0) == (half * 8 + slot + 16 * (me % 8)))
    high = jnp.where(to_chip, lax.shift_right_logical(value, 4).astype(F32), 0.0).astype(BF16)
    low = jnp.where(to_chip, (value & 15).astype(F32), 0.0).astype(BF16)
    meta = 16.0 * dot_t(high, lanes) + dot_t(low, lanes)
    for n in range(64):
        meta_s[n] = meta[n : n + 1, :]

    emb_copy.wait()
    rows = emb[...]
    scale = lax.rsqrt(jnp.sum(rows * rows, axis=1, keepdims=True) + 1e-06)
    unit[...] = (rows * scale).astype(BF16)
    for a in range(8):
        take = ones(iota((128, ROWS), 0) + 128 * a == line)
        packed = dot(take, unit[...]).astype(BF16)
        sbuf[0, pl.ds(128 * a, 128), :] = packed[:, :HALF]
        sbuf[1, pl.ds(128 * a, 128), :] = packed[:, HALF:]

    @pl.when(lead & jnp.logical_not(root))
    def _():
        pl.semaphore_wait(barrier, 15)
        greet(2, 2, 3, 0)
        pl.semaphore_wait(barrier, 1)

    @pl.when(root)
    def _():
        pl.semaphore_wait(barrier, 22)
        for j in range(7, 0, -1):
            greet((2 + 2 * (j // 4)) % 4, (2 + 2 * (j // 2 % 2)) % 4, (3 + 2 * (j % 2)) % 4, 0)

    @pl.when(lead)
    def _():
        for j in range(15, 0, -1):
            greet(x + j // 8, y + j // 4 % 2, z - j // 2 % 2, j % 2)

    @pl.when(jnp.logical_not(lead))
    def _():
        pl.semaphore_wait(barrier, 1)

    def send_rows(e, _):
        tx, ty, tz, tk = relative(e)
        n = tx * 16 + ty * 4 + tz
        pltpu.make_async_remote_copy(
            src_ref=sbuf.at[tk, pl.ds(pl.multiple_of(16 * n, 16), 16)],
            dst_ref=rb.at[pl.ds(pl.multiple_of(16 * me, 16), 16)],
            send_sem=row_s, recv_sem=row_r,
            device_id=(2 * tx + tk, 4 * ty + tz), device_id_type=MESH,
        ).start()
        return _

    def send_meta(e, _):
        tx, ty, tz, tk = relative(e)
        n = tx * 16 + ty * 4 + tz
        pltpu.make_async_remote_copy(
            src_ref=meta_s.at[n], dst_ref=meta_r.at[me],
            send_sem=meta_ss, recv_sem=meta_rr,
            device_id=(2 * tx + tk, 4 * ty + tz), device_id_type=MESH,
        ).start()
        return _

    ids_copy.wait()
    at_home = y // 2 == k

    def send_ids(j, carry):
        hy, hz, hk = 2 * k + j // 8, (j // 2) % 4, j % 2
        to_self = (hy == y) & (hz == z) & (hk == k)

        @pl.when(to_self)
        def _():
            pltpu.make_async_copy(ids_ref, labs.at[col], lab_r).start()

        @pl.when(jnp.logical_not(to_self))
        def _():
            pltpu.make_async_remote_copy(
                src_ref=ids_ref, dst_ref=labs.at[col],
                send_sem=lab_s, recv_sem=lab_r,
                device_id=(2 * x + hk, 4 * hy + hz), device_id_type=MESH,
            ).start()

        return carry

    lax.fori_loop(1, 49, send_rows, 0)
    lax.fori_loop(0, 16, send_ids, 0)
    lax.fori_loop(1, DEVS, send_meta, 0)
    lax.fori_loop(49, DEVS, send_rows, 0)
    own_copy = pltpu.make_async_copy(
        sbuf.at[k, pl.ds(pl.multiple_of(16 * chip, 16), 16)],
        rb.at[pl.ds(pl.multiple_of(16 * me, 16), 16)], own_sem,
    )
    own_copy.start()
    meta_r[me] = meta_s[chip]

    pltpu.make_async_copy(labs, labs, lab_r).wait()
    large = labs[7, :, 0:1]
    first = jnp.where(share < 6, share, 2 * share - 6)
    second = jnp.where(share < 6, share + 10, 2 * share - 5)
    is_large = labs[first] == large
    eye = ones(iota((ROWS, ROWS), 0) == iota((ROWS, ROWS), 1))

    def column(r):
        return dot_t(eye, jnp.broadcast_to(r, (8, ROWS)).astype(BF16))[:, 0:1]

    rest_ids = jnp.where(is_large, labs[second], labs[first]).astype(F32)
    rest_col = column(rest_ids)
    large_col = column(jnp.where(is_large, 1.0, 0.0))
    index_col = iota((ROWS, 1), 0).astype(F32) + 1.0
    key_large = index_col + 512.0 * (1.0 - large_col)
    key_rest = index_col + 512.0 * large_col

    pltpu.make_async_copy(meta_r.at[pl.ds(0, DEVS - 1)], meta_r.at[pl.ds(0, DEVS - 1)], meta_rr).wait()
    for a in range(16):
        r = meta_r[8 * a]
        for i in range(1, 8):
            r = r + meta_r[8 * a + i]
        q[0:ROWS, pl.ds(128 * a, 128)] = ones(key_large == r)
        q[ROWS : 2 * ROWS, pl.ds(128 * a, 128)] = ones(key_rest == r)

    own_copy.wait()
    pltpu.make_async_copy(rb.at[pl.ds(0, 16 * (DEVS - 1))], rb.at[pl.ds(0, 16 * (DEVS - 1))], row_r).wait()

    def along(bit):
        ny = y + 1 - 2 * (y % 2) if bit == 2 else y
        nz = z + 1 - 2 * (z % 2) if bit == 0 else 3 - z if bit == 1 else z
        return (2 * x + k, 4 * ny + nz)

    def between(src, dst, n, send, recv, device):
        return pltpu.make_async_remote_copy(
            src_ref=xs.at[k, pl.ds(src, n)], dst_ref=xs.at[k, pl.ds(dst, n)],
            send_sem=send, recv_sem=recv, device_id=device, device_id_type=MESH,
        )

    sibling = (2 * x + 1 - k, col)

    def pair_copy(i, start, n):
        return between(start, start, n, pair_s.at[i], pair_r.at[i], sibling)

    def block_copy(bit, c):
        at, n = CHUNKS[c]
        src = pl.multiple_of(pick(p, SEND[bit]) + at, 16)
        return between(src, SLOT[1 + bit] + at, n, ici_s.at[bit, c], ici_r.at[bit, c], along(bit))

    n_chunks = len(CHUNKS)
    copies = [[block_copy(bit, c) for c in range(n_chunks)] for bit in range(3)]
    block_pairs = [[pair_copy(3 + bit * n_chunks + c, SLOT[1 + bit] + CHUNKS[c][0], CHUNKS[c][1]) for c in range(n_chunks)] for bit in range(3)]
    own_pair, second_pair = pair_copy(0, 0, ROWS), pair_copy(1, SECOND, ROWS)
    patch_pair, head_pair = pair_copy(2, PATCH, QUARTER), pair_copy(3 + 3 * n_chunks, HEAD, HEAD_ROWS)
    has_patch = (p != 1) & (p != 4) & (p != 5)
    has_head = (p != 2) & (p != 6) & (p != 4)
    gives_head = (p != 2) & (p != 6) & (p != 0)

    def patch_copy(i):
        frm, to, bit, src = PATCHES[i]
        return between(src, PATCH, QUARTER, patch_s.at[i % 2], patch_r, along(bit))

    def head_copy(bit):
        return between(SECOND, HEAD, HEAD_ROWS, head_s, head_r, along(bit))

    for c in range(n_chunks):
        at, n = CHUNKS[c]
        xs[k, pl.ds(at, n), :] = dot(q[at : at + n, :], rb[...]).astype(BF16)

        @pl.when(p != 6)
        def _():
            copies[0][c].start()

        @pl.when(p != 2)
        def _():
            copies[1][c].start()

        @pl.when(p == 6)
        def _():
            copies[2][c].start()

        if at + n == 2 * QUARTER:
            @pl.when(p == 4)
            def _():
                patch_copy(0).start()

    own_pair.start()
    xs[k, pl.ds(SECOND, ROWS), :] = dot(q[ROWS : 2 * ROWS, :], rb[...]).astype(BF16)
    for c in range(n_chunks):
        @pl.when(p == 6)
        def _():
            copies[0][c].start()

        @pl.when(p == 2)
        def _():
            copies[1][c].start()
            copies[2][c].start()

    second_pair.start()
    for v, bit in ((1, 0), (3, 1), (7, 2), (5, 1), (4, 0)):
        @pl.when(p == v)
        def _():
            head_copy(bit).start()

    mine = pl.multiple_of(QUARTER * k, QUARTER)
    starts = SLOT + (SECOND,)

    def columns_of(s):
        return pl.multiple_of(starts[s] + mine, QUARTER)

    def tile(j, nj, i, ni):
        return dot_t(xs[0, pl.ds(j, nj), :], xs[0, pl.ds(i, ni), :]) + dot_t(
            xs[1, pl.ds(j, nj), :], xs[1, pl.ds(i, ni), :]
        )

    def top(t):
        return jnp.max(t, axis=0, keepdims=True)

    def meet(s, j, nj):
        t = tile(j, nj, columns_of(s), QUARTER)
        if j <= starts[s] < j + nj:
            t = jnp.where(iota((nj, QUARTER), 0) == iota((nj, QUARTER), 1) + (starts[s] - j + mine), -1.0, t)
        acc[s] = jnp.maximum(acc[s], top(t))

    ob[...] = jnp.full(ob.shape, -1.0, F32)
    acc[...] = jnp.full(acc.shape, -1.0, F32)
    rest_row = jnp.where(k == 0, rest_ids[:, :QUARTER], rest_ids[:, QUARTER:])

    own_pair.wait_recv()
    meet(0, 0, ROWS)
    for c in range(n_chunks):
        copies[0][c].wait_recv()
        copies[1][c].wait_recv()

        @pl.when(jnp.logical_not(large_only))
        def _():
            copies[2][c].start()

        block_pairs[0][c].start()
        block_pairs[1][c].start()
        if CHUNKS[c][0] + CHUNKS[c][1] == QUARTER:
            @pl.when(p == 6)
            def _():
                patch_copy(1).start()

            @pl.when(p == 2)
            def _():
                patch_copy(3).start()

    @pl.when(p == 6)
    def _():
        patch_copy(2).start()

    @pl.when(p == 2)
    def _():
        patch_copy(4).start()

    second_pair.wait_recv()
    t = tile(SECOND, ROWS, columns_of(4), QUARTER)
    own = iota((ROWS, QUARTER), 0) == iota((ROWS, QUARTER), 1) + mine
    acc[4] = top(jnp.where((rest_col == rest_row) & jnp.logical_not(own), t, -1.0))
    for c in range(n_chunks):
        block_pairs[0][c].wait_recv()
        block_pairs[1][c].wait_recv()
    meet(0, ROWS, 2 * ROWS)
    meet(1, 0, 3 * ROWS)
    meet(2, 0, 3 * ROWS)

    @pl.when(large_only)
    def _():
        for s in range(3):
            meet(s, SECOND, ROWS)
        meet(4, 0, 3 * ROWS)

    for c in range(n_chunks - 1):
        copies[2][c].wait_recv()
        block_pairs[2][c].start()
    for c in range(n_chunks - 2):
        block_pairs[2][c].wait_recv()
    for s in range(3):
        meet(s, SLOT[3], QUARTER)

    @pl.when(large_only)
    def _():
        meet(4, SLOT[3], QUARTER)

    copies[2][n_chunks - 1].wait_recv()
    block_pairs[2][n_chunks - 1].start()

    @pl.when(has_head)
    def _():
        head_copy(0).wait_recv()
        head_pair.start()

    @pl.when(has_patch)
    def _():
        patch_copy(0).wait_recv()
        patch_pair.start()

    for c in range(n_chunks - 2, n_chunks):
        block_pairs[2][c].wait_recv()
    for s in range(3):
        meet(s, SLOT[3] + QUARTER, QUARTER)
    meet(3, 0, 4 * ROWS)

    @pl.when(large_only)
    def _():
        meet(4, SLOT[3] + QUARTER, QUARTER)
        meet(3, SECOND, ROWS)

    def raise_to(b, at, n, v):
        ob[b, :, pl.ds(at, n)] = jnp.maximum(ob[b, :, pl.ds(at, n)], v)

    @pl.when(has_head)
    def _():
        head_pair.wait_recv()
        nxt = labs[share + 1]
        head_ids = jnp.where(nxt == large, labs[share + 11], nxt).astype(F32)
        head_col = column(head_ids)[:HEAD_ROWS]
        t = tile(HEAD, HEAD_ROWS, columns_of(4), QUARTER)
        acc[4] = jnp.maximum(acc[4], top(jnp.where(head_col == rest_row, t, -1.0)))
        t = tile(columns_of(4), QUARTER, HEAD, HEAD_ROWS)
        some_col = jnp.where(k == 0, rest_col[:QUARTER], rest_col[QUARTER:])
        m = top(jnp.where(some_col == head_ids[:, :HEAD_ROWS], t, -1.0))
        m = jnp.concatenate([m, jnp.full((1, ROWS - HEAD_ROWS), -1.0, F32)], axis=1)
        raise_to(share + 1, 0, ROWS, jnp.where(nxt == large, -1.0, m))
        raise_to(share + 11, 0, ROWS, jnp.where(nxt == large, m, -1.0))

    @pl.when(has_patch)
    def _():
        patch_pair.wait_recv()
        patch_cols = pl.multiple_of(PATCH + 128 * k, 128)

        def meets(start):
            t = tile(PATCH, QUARTER, pl.multiple_of(start + mine, QUARTER), QUARTER)
            s = jnp.where(start == SECOND, 4, start // ROWS)
            acc[s] = jnp.maximum(acc[s], top(t))
            return top(tile(pl.multiple_of(start, ROWS), ROWS, patch_cols, 128))

        at = pl.multiple_of(QUARTER * pick(p, PATCH_HALF) + 128 * k, 128)
        v = pick(p, PATCH_BLOCK)
        here = labs[v, :, pl.ds(at, 128)] == large

        def give(m):
            raise_to(v, at, 128, jnp.where(here, m, -1.0))
            raise_to(v + 10, at, 128, jnp.where(here, -1.0, m))

        give(meets(pick(p, PATCH_MEETS)))

        @pl.when(p == 2)
        def _():
            give(meets(jnp.int32(SLOT[2])))

    for s in range(4):
        v = pick(p, tuple(h[s] for h in HELD))
        here = labs[v, :, pl.ds(mine, QUARTER)] == large
        raise_to(v, mine, QUARTER, jnp.where(here, acc[s], -1.0))

        @pl.when(v < 6)
        def _():
            raise_to(v + 10, mine, QUARTER, jnp.where(here, -1.0, acc[s]))

    here = labs[first, :, pl.ds(mine, QUARTER)] == large
    raise_to(second, mine, QUARTER, jnp.where(here, acc[4], -1.0))
    raise_to(first, mine, QUARTER, jnp.where(here, -1.0, acc[4]))

    def send_best(b, carry):
        to_self = at_home & (b == col)

        @pl.when(to_self)
        def _():
            pltpu.make_async_copy(ob.at[b], fin.at[p * 2 + k], fin_r).start()

        @pl.when(jnp.logical_not(to_self))
        def _():
            pltpu.make_async_remote_copy(
                src_ref=ob.at[b], dst_ref=fin.at[p * 2 + k],
                send_sem=fin_s, recv_sem=fin_r, device_id=(group, b), device_id_type=MESH,
            ).start()

        return carry

    lax.fori_loop(0, 16, send_best, 0)

    pltpu.make_async_copy(sbuf.at[0, pl.ds(0, 1008)], sbuf.at[0, pl.ds(0, 1008)], row_s).wait()
    pltpu.make_async_copy(sbuf.at[0], sbuf.at[0], row_s).wait()
    pltpu.make_async_copy(meta_r.at[pl.ds(0, DEVS - 1)], meta_r.at[pl.ds(0, DEVS - 1)], meta_ss).wait()
    for per_bit in copies + block_pairs:
        for cp in per_bit:
            cp.wait_send()
    own_pair.wait_send()
    second_pair.wait_send()

    @pl.when(has_head)
    def _():
        head_pair.wait_send()

    @pl.when(has_patch)
    def _():
        patch_pair.wait_send()

    @pl.when(gives_head)
    def _():
        head_copy(0).wait_send()

    for v, which in ((4, (0,)), (6, (1, 2)), (2, (3, 4))):
        @pl.when(p == v)
        def _():
            for i in which:
                patch_copy(i).wait_send()

    @pl.when(at_home)
    def _():
        pltpu.make_async_copy(labs.at[pl.ds(0, 15)], labs.at[pl.ds(0, 15)], lab_s).wait()
        pltpu.make_async_copy(fin.at[pl.ds(0, 15)], fin.at[pl.ds(0, 15)], fin_s).wait()

    @pl.when(jnp.logical_not(at_home))
    def _():
        pltpu.make_async_copy(labs, labs, lab_s).wait()
        pltpu.make_async_copy(fin, fin, fin_s).wait()

    pltpu.make_async_copy(fin, fin, fin_r).wait()
    best = fin[0]
    for i in range(1, 16):
        best = jnp.maximum(best, fin[i])
    out_ref[...] = best


def shards(embeddings, dest_pos, cluster_ids):
    dma, n_pairs = pltpu.SemaphoreType.DMA, 4 + 3 * len(CHUNKS)
    return pl.pallas_call(
        kernel,
        out_shape=jax.ShapeDtypeStruct((1, ROWS), F32),
        in_specs=[
            pl.BlockSpec(memory_space=pltpu.HBM),
            pl.BlockSpec(memory_space=pltpu.HBM),
            pl.BlockSpec(memory_space=pltpu.HBM),
        ],
        out_specs=pl.BlockSpec(memory_space=pltpu.VMEM),
        scratch_shapes=[
            pltpu.VMEM((ROWS, WIDTH), F32),
            pltpu.VMEM((1, ROWS), I32),
            pltpu.VMEM((1, ROWS), I32),
            pltpu.VMEM((ROWS, WIDTH), BF16),
            pltpu.VMEM((2, 1024, HALF), BF16),
            pltpu.VMEM((16 * DEVS, HALF), BF16),
            pltpu.VMEM((64, 1, 128), F32),
            pltpu.VMEM((DEVS, 1, 128), F32),
            pltpu.VMEM((16, 1, ROWS), I32),
            pltpu.VMEM((2 * ROWS, 16 * DEVS), BF16),
            pltpu.VMEM((2, X_ROWS, HALF), BF16),
            pltpu.VMEM((5, 1, QUARTER), F32),
            pltpu.VMEM((16, 1, ROWS), F32),
            pltpu.VMEM((16, 1, ROWS), F32),
            dma, dma, dma, dma, dma, dma, dma, dma, dma, dma,
            dma((3, len(CHUNKS))), dma((3, len(CHUNKS))), dma((n_pairs,)), dma((n_pairs,)),
            dma((2,)), dma, dma, dma, dma, dma,
        ],
        compiler_params=pltpu.CompilerParams(
            collective_id=0, has_side_effects=True, vmem_limit_bytes=62 * 2**20
        ),
        name="best_match",
    )(embeddings, dest_pos.reshape(1, ROWS), cluster_ids)


def solution(mesh):
    return jax.shard_map(
        shards,
        mesh=mesh,
        in_specs=(P(("row", "col"), None), P(("row", "col")), P("row", "col")),
        out_specs=P("row", "col"),
        check_vma=False,
    )
```

time: 86.9 us -> 76.2 us (0.88)
  Pallas kernels: 83.1 us -> 74.7 us
  local copies, waits for them, and re-layouts: 3.53 us -> 1.26 us
    pallas_call x1, Pallas kernels: 83.1 us -> 74.7 us  [shards(): pl.pallas_call(kernel, out_shape=jax.ShapeDtypeStruct((1, ROWS), F32), in...]
    unnamed x7 -> x1, local copies, waits for them, and re-layouts: 3.53 us -> 1.26 us
where the time goes in v2:
time: 76.2 us; the launch traced here: 76 us
  Pallas kernels  74.7 us (98%)
  local copies, waits for them, and re-layouts  1.26 us (2%)
    pallas_call x1, Pallas kernels, shards(): pl.pallas_call(kernel, out_shape=jax.ShapeDtypeStruct((1, ROWS), F32), in...  74.7 us

profile of v2, /device:TPU:1, one launch (start us, length us, event | category | flops | bytes accessed | tf_op | source)
XLA Modules:
  0.0 76.0 jit_solution(12022513845881074043)
XLA Ops:
  0.0 74.7 %best_match.1 = f32[1,512]{1,0:T(1,128)} custom-call(f32[512,1024]{1,0:T(8,128)} %emb_hbm.1, s32[1,512]{1,0:T(1,128)} %bitcast.1, s32[1,512]{1,0:T(1,128)} %ids_hbm.1), custom_call_target="tpu_custom_call" | custom-call | tf_op jit(solution)/shard_map/best_match/pallas_call | solution.py:541
  74.8 1.3 %copy.5 = f32[1,512]{1,0:T(1,128)} copy(f32[1,512]{1,0:T(1,128)} %best_match.1) | data formatting | bytes 4096

commit v3 on v2

--- a/solution.py
+++ b/solution.py
@@ -30,7 +30,8 @@
 PATCH_HALF = (1, 0, 0, 0, 0, 0, 1, 1)
 PATCH_MEETS = (0, 0, 0, 1536, 0, 0, SECOND, 1536)
 PATCHES = ((4, 0, 2, 256), (6, 2, 2, 1024), (6, 7, 0, 1280), (2, 3, 0, 1024), (2, 6, 2, 1280))
-CHUNKS = ((0, 64), (64, 64), (128, 128), (256, 128), (384, 128))
+CHUNKS = ((0, 128), (128, 128), (256, 128), (384, 128))
+STRIDE, INVERSE, EARLY = 45, 37, 48
 
 
 def pick(p, table):
@@ -59,14 +60,13 @@
 
 def kernel(
     emb_hbm, dest_hbm, ids_hbm, out_ref,
-    emb, dest_ref, ids_ref, unit, sbuf, rb, meta_s, meta_r, labs, q, xs, acc, ob, fin,
-    emb_sem, dest_sem, ids_sem, own_sem, row_s, row_r, meta_ss, meta_rr, lab_s, lab_r,
+    emb, dest_ref, ids_ref, unit, sbuf, rb, part, meta_s, meta_r, labs, q, xs, acc, last, ob, fin,
+    emb_sem, dest_sem, ids_sem, own_sem, row_s, row_r, meta_ss, meta_rr, meta_ps, meta_pr, lab_s, lab_r,
     ici_s, ici_r, pair_s, pair_r, patch_s, patch_r, head_s, head_r, fin_s, fin_r,
 ):
     row, col = lax.axis_index("row"), lax.axis_index("col")
     x, k, y, z = row // 2, row % 2, col // 4, col % 4
     chip = x * 16 + y * 4 + z
-    me = chip * 2 + k
     group = 2 * x + y // 2
     p = (y % 2) * 4 + (z // 2) * 2 + (z // 2 + z) % 2
     share = pick(p, CHIP)
@@ -79,22 +79,20 @@
     ids_copy = pltpu.make_async_copy(ids_hbm, ids_ref, ids_sem)
     ids_copy.start()
 
-    def relative(e):
-        off = (e * 45) % DEVS
-        dx, dy, dz, dk = off // 32, (off // 8) % 4, (off // 2) % 4, off % 2
-        return (x + dx) % 4, (y + dy) % 4, (z + dz) % 4, (k + dk) % 2
+    def relative(n):
+        off = (n * STRIDE) % 64
+        return (x + off // 16) % 4, (y + off // 4 % 4) % 4, (z + off % 4) % 4
 
     barrier = pltpu.get_barrier_semaphore()
 
     def greet(tx, ty, tz, tk):
         pl.semaphore_signal(barrier, inc=1, device_id=(2 * tx + tk, 4 * ty + tz), device_id_type=MESH)
 
-    lead = (x % 2 == 0) & (y % 2 == 0) & (z % 2 == 1) & (k == 0)
-    root = (x == 2) & (y == 2) & (z == 3) & (k == 0)
-
-    @pl.when(jnp.logical_not(lead))
-    def _():
-        greet(x - x % 2, y - y % 2, z - z % 2 + 1, 0)
+    lead = (x % 2 == 0) & (y % 2 == 0) & (z % 2 == 0)
+
+    @pl.when(jnp.logical_not(lead & (k == 0)))
+    def _():
+        greet(x - x % 2, y - y % 2, z - z % 2, 0)
 
     dest_copy.wait()
     dest = dest_ref[...]
@@ -108,6 +106,7 @@
     ty = 2 * (g & 1) + lax.shift_right_logical(vert, 2)
     tz = (vert & 2) + (lax.shift_right_logical(vert, 1) + vert & 1)
     tchip = tx * 16 + ty * 4 + tz
+    turn = (((tx - x) & 3) * 16 + ((ty - y) & 3) * 4 + ((tz - z) & 3)) * INVERSE & 3
     tb = tchip * 2 + half
     hot = iota((DEVS, ROWS), 0) == tb
     before = ones(iota((ROWS, ROWS), 0) < iota((ROWS, ROWS), 1))
@@ -117,7 +116,7 @@
 
     value = place + 1 + 512 * half
     to_chip = iota((64, ROWS), 0) == tchip
-    lanes = ones(iota((128, ROWS), 0) == (half * 8 + slot + 16 * (me % 8)))
+    lanes = ones(iota((128, ROWS), 0) == (half * 8 + slot + 16 * (2 * turn + k)))
     high = jnp.where(to_chip, lax.shift_right_logical(value, 4).astype(F32), 0.0).astype(BF16)
     low = jnp.where(to_chip, (value & 15).astype(F32), 0.0).astype(BF16)
     meta = 16.0 * dot_t(high, lanes) + dot_t(low, lanes)
@@ -134,47 +133,42 @@
         sbuf[0, pl.ds(128 * a, 128), :] = packed[:, :HALF]
         sbuf[1, pl.ds(128 * a, 128), :] = packed[:, HALF:]
 
-    @pl.when(lead & jnp.logical_not(root))
+    @pl.when(lead & (k == 0))
     def _():
         pl.semaphore_wait(barrier, 15)
-        greet(2, 2, 3, 0)
+        for j in range(7, -1, -1):
+            greet((x + 2 * (j // 4)) % 4, (y + 2 * (j // 2 % 2)) % 4, (z + 2 * (j % 2)) % 4, 1)
         pl.semaphore_wait(barrier, 1)
 
-    @pl.when(root)
-    def _():
-        pl.semaphore_wait(barrier, 22)
-        for j in range(7, 0, -1):
-            greet((2 + 2 * (j // 4)) % 4, (2 + 2 * (j // 2 % 2)) % 4, (3 + 2 * (j % 2)) % 4, 0)
-
-    @pl.when(lead)
-    def _():
+    @pl.when(lead & (k == 1))
+    def _():
+        pl.semaphore_wait(barrier, 8)
         for j in range(15, 0, -1):
-            greet(x + j // 8, y + j // 4 % 2, z - j // 2 % 2, j % 2)
+            greet(x + j // 8, y + j // 4 % 2, z + j // 2 % 2, (1 + j) % 2)
 
     @pl.when(jnp.logical_not(lead))
     def _():
         pl.semaphore_wait(barrier, 1)
 
-    def send_rows(e, _):
-        tx, ty, tz, tk = relative(e)
-        n = tx * 16 + ty * 4 + tz
+    def send_rows(e, carry):
+        n, tk = e // 2, e % 2
+        tx, ty, tz = relative(n)
         pltpu.make_async_remote_copy(
-            src_ref=sbuf.at[tk, pl.ds(pl.multiple_of(16 * n, 16), 16)],
-            dst_ref=rb.at[pl.ds(pl.multiple_of(16 * me, 16), 16)],
-            send_sem=row_s, recv_sem=row_r,
+            src_ref=sbuf.at[tk, pl.ds(pl.multiple_of(16 * (tx * 16 + ty * 4 + tz), 16), 16)],
+            dst_ref=rb.at[pl.ds(pl.multiple_of(16 * (2 * n + k), 16), 16)],
+            send_sem=row_s, recv_sem=row_r.at[n // EARLY],
             device_id=(2 * tx + tk, 4 * ty + tz), device_id_type=MESH,
         ).start()
-        return _
-
-    def send_meta(e, _):
-        tx, ty, tz, tk = relative(e)
-        n = tx * 16 + ty * 4 + tz
+        return carry
+
+    def send_meta(n, carry):
+        tx, ty, tz = relative(n)
         pltpu.make_async_remote_copy(
-            src_ref=meta_s.at[n], dst_ref=meta_r.at[me],
+            src_ref=meta_s.at[tx * 16 + ty * 4 + tz], dst_ref=meta_r.at[64 * k + n],
             send_sem=meta_ss, recv_sem=meta_rr,
-            device_id=(2 * tx + tk, 4 * ty + tz), device_id_type=MESH,
+            device_id=(2 * tx + k, 4 * ty + tz), device_id_type=MESH,
         ).start()
-        return _
+        return carry
 
     ids_copy.wait()
     at_home = y // 2 == k
@@ -197,16 +191,27 @@
 
         return carry
 
-    lax.fori_loop(1, 49, send_rows, 0)
+    lax.fori_loop(2, 50, send_rows, 0)
     lax.fori_loop(0, 16, send_ids, 0)
-    lax.fori_loop(1, DEVS, send_meta, 0)
-    lax.fori_loop(49, DEVS, send_rows, 0)
-    own_copy = pltpu.make_async_copy(
-        sbuf.at[k, pl.ds(pl.multiple_of(16 * chip, 16), 16)],
-        rb.at[pl.ds(pl.multiple_of(16 * me, 16), 16)], own_sem,
+    lax.fori_loop(1, 64, send_meta, 0)
+    lax.fori_loop(50, DEVS, send_rows, 0)
+    sibling = (2 * x + 1 - k, col)
+    own_rows = pl.ds(pl.multiple_of(16 * chip, 16), 16)
+    own_slot = pl.ds(pl.multiple_of(16 * k, 16), 16)
+    sibling_copy = pltpu.make_async_remote_copy(
+        src_ref=sbuf.at[1 - k, own_rows], dst_ref=rb.at[own_slot],
+        send_sem=row_s, recv_sem=row_r.at[0], device_id=sibling, device_id_type=MESH,
     )
+    sibling_copy.start()
+    own_copy = pltpu.make_async_copy(sbuf.at[k, own_rows], rb.at[own_slot], own_sem)
     own_copy.start()
-    meta_r[me] = meta_s[chip]
+    meta_r[64 * k] = meta_s[chip]
+    pltpu.make_async_copy(meta_s.at[pl.ds(0, 63)], meta_s.at[pl.ds(0, 63)], meta_rr).wait()
+    meta_pair = pltpu.make_async_remote_copy(
+        src_ref=meta_r.at[pl.ds(pl.multiple_of(64 * k, 64), 64)], dst_ref=meta_r.at[pl.ds(pl.multiple_of(64 * k, 64), 64)],
+        send_sem=meta_ps, recv_sem=meta_pr, device_id=sibling, device_id_type=MESH,
+    )
+    meta_pair.start()
 
     pltpu.make_async_copy(labs, labs, lab_r).wait()
     large = labs[7, :, 0:1]
@@ -225,16 +230,19 @@
     key_large = index_col + 512.0 * (1.0 - large_col)
     key_rest = index_col + 512.0 * large_col
 
-    pltpu.make_async_copy(meta_r.at[pl.ds(0, DEVS - 1)], meta_r.at[pl.ds(0, DEVS - 1)], meta_rr).wait()
+    meta_pair.wait_recv()
     for a in range(16):
-        r = meta_r[8 * a]
-        for i in range(1, 8):
-            r = r + meta_r[8 * a + i]
+        r = meta_r[4 * a] + meta_r[64 + 4 * a]
+        for i in range(1, 4):
+            r = r + (meta_r[4 * a + i] + meta_r[64 + 4 * a + i])
         q[0:ROWS, pl.ds(128 * a, 128)] = ones(key_large == r)
         q[ROWS : 2 * ROWS, pl.ds(128 * a, 128)] = ones(key_rest == r)
 
     own_copy.wait()
-    pltpu.make_async_copy(rb.at[pl.ds(0, 16 * (DEVS - 1))], rb.at[pl.ds(0, 16 * (DEVS - 1))], row_r).wait()
+    early = 32 * EARLY
+    pltpu.make_async_copy(rb.at[pl.ds(0, early - 16)], rb.at[pl.ds(0, early - 16)], row_r.at[0]).wait()
+    part[...] = dot(q[:, 0:early], rb[0:early, :])
+    pltpu.make_async_copy(rb.at[pl.ds(early, 2048 - early)], rb.at[pl.ds(early, 2048 - early)], row_r.at[1]).wait()
 
     def along(bit):
         ny = y + 1 - 2 * (y % 2) if bit == 2 else y
@@ -246,8 +254,6 @@
             src_ref=xs.at[k, pl.ds(src, n)], dst_ref=xs.at[k, pl.ds(dst, n)],
             send_sem=send, recv_sem=recv, device_id=device, device_id_type=MESH,
         )
-
-    sibling = (2 * x + 1 - k, col)
 
     def pair_copy(i, start, n):
         return between(start, start, n, pair_s.at[i], pair_r.at[i], sibling)
@@ -273,10 +279,7 @@
     def head_copy(bit):
         return between(SECOND, HEAD, HEAD_ROWS, head_s, head_r, along(bit))
 
-    for c in range(n_chunks):
-        at, n = CHUNKS[c]
-        xs[k, pl.ds(at, n), :] = dot(q[at : at + n, :], rb[...]).astype(BF16)
-
+    def own_sends(c):
         @pl.when(p != 6)
         def _():
             copies[0][c].start()
@@ -289,13 +292,23 @@
         def _():
             copies[2][c].start()
 
-        if at + n == 2 * QUARTER:
+        if CHUNKS[c][0] + CHUNKS[c][1] == ROWS:
             @pl.when(p == 4)
             def _():
                 patch_copy(0).start()
 
+    def unpacked(at, n):
+        rows = slice(at, at + n)
+        return (part[rows, :] + dot(q[rows, early:], rb[early:, :])).astype(BF16)
+
+    for at in range(0, ROWS, QUARTER):
+        xs[k, pl.ds(at, QUARTER), :] = unpacked(at, QUARTER)
+        for c in range(n_chunks):
+            if at <= CHUNKS[c][0] < at + QUARTER:
+                own_sends(c)
+
     own_pair.start()
-    xs[k, pl.ds(SECOND, ROWS), :] = dot(q[ROWS : 2 * ROWS, :], rb[...]).astype(BF16)
+    xs[k, pl.ds(SECOND, ROWS), :] = unpacked(ROWS, ROWS)
     for c in range(n_chunks):
         @pl.when(p == 6)
         def _():
@@ -331,6 +344,40 @@
         if j <= starts[s] < j + nj:
             t = jnp.where(iota((nj, QUARTER), 0) == iota((nj, QUARTER), 1) + (starts[s] - j + mine), -1.0, t)
         acc[s] = jnp.maximum(acc[s], top(t))
+
+    def across(t):
+        m = t[:, :128]
+        for i in range(128, t.shape[1], 128):
+            m = jnp.maximum(m, t[:, i : i + 128])
+        return jnp.max(jnp.transpose(m), axis=0, keepdims=True)
+
+    def late(at):
+        rows, lanes = SLOT[3] + at, pl.ds(at, QUARTER)
+
+        def against(s):
+            t = tile(rows, QUARTER, columns_of(s), QUARTER)
+            acc[s] = jnp.maximum(acc[s], top(t))
+            return t
+
+        t = jnp.maximum(jnp.maximum(against(0), against(1)), against(2))
+        last[:, lanes] = across(t)
+
+        @pl.when(large_only)
+        def _():
+            last[:, lanes] = jnp.maximum(last[:, lanes], across(against(4)))
+
+        @pl.when(k == at // QUARTER)
+        def _():
+            t = tile(rows, QUARTER, rows, QUARTER)
+            same = iota((QUARTER, QUARTER), 0) == iota((QUARTER, QUARTER), 1)
+            last[:, lanes] = jnp.maximum(last[:, lanes], top(jnp.where(same, -1.0, t)))
+
+        if at:
+            @pl.when(k == 0)
+            def _():
+                t = tile(rows, QUARTER, SLOT[3], QUARTER)
+                last[:, 0:QUARTER] = jnp.maximum(last[:, 0:QUARTER], top(t))
+                last[:, lanes] = jnp.maximum(last[:, lanes], across(t))
 
     ob[...] = jnp.full(ob.shape, -1.0, F32)
     acc[...] = jnp.full(acc.shape, -1.0, F32)
@@ -385,15 +432,10 @@
     for c in range(n_chunks - 1):
         copies[2][c].wait_recv()
         block_pairs[2][c].start()
-    for c in range(n_chunks - 2):
-        block_pairs[2][c].wait_recv()
-    for s in range(3):
-        meet(s, SLOT[3], QUARTER)
-
-    @pl.when(large_only)
-    def _():
-        meet(4, SLOT[3], QUARTER)
-
+    for c in range(n_chunks):
+        if sum(CHUNKS[c]) <= QUARTER:
+            block_pairs[2][c].wait_recv()
+    late(0)
     copies[2][n_chunks - 1].wait_recv()
     block_pairs[2][n_chunks - 1].start()
 
@@ -407,16 +449,10 @@
         patch_copy(0).wait_recv()
         patch_pair.start()
 
-    for c in range(n_chunks - 2, n_chunks):
-        block_pairs[2][c].wait_recv()
-    for s in range(3):
-        meet(s, SLOT[3] + QUARTER, QUARTER)
-    meet(3, 0, 4 * ROWS)
-
-    @pl.when(large_only)
-    def _():
-        meet(4, SLOT[3] + QUARTER, QUARTER)
-        meet(3, SECOND, ROWS)
+    for c in range(n_chunks):
+        if sum(CHUNKS[c]) > QUARTER:
+            block_pairs[2][c].wait_recv()
+    late(QUARTER)
 
     def raise_to(b, at, n, v):
         ob[b, :, pl.ds(at, n)] = jnp.maximum(ob[b, :, pl.ds(at, n)], v)
@@ -427,33 +463,28 @@
         nxt = labs[share + 1]
         head_ids = jnp.where(nxt == large, labs[share + 11], nxt).astype(F32)
         head_col = column(head_ids)[:HEAD_ROWS]
-        t = tile(HEAD, HEAD_ROWS, columns_of(4), QUARTER)
-        acc[4] = jnp.maximum(acc[4], top(jnp.where(head_col == rest_row, t, -1.0)))
-        t = tile(columns_of(4), QUARTER, HEAD, HEAD_ROWS)
-        some_col = jnp.where(k == 0, rest_col[:QUARTER], rest_col[QUARTER:])
-        m = top(jnp.where(some_col == head_ids[:, :HEAD_ROWS], t, -1.0))
-        m = jnp.concatenate([m, jnp.full((1, ROWS - HEAD_ROWS), -1.0, F32)], axis=1)
+        t = jnp.where(head_col == rest_row, tile(HEAD, HEAD_ROWS, columns_of(4), QUARTER), -1.0)
+        acc[4] = jnp.maximum(acc[4], top(t))
+        m = across(jnp.concatenate([t, jnp.full((ROWS - HEAD_ROWS, QUARTER), -1.0, F32)], axis=0))
         raise_to(share + 1, 0, ROWS, jnp.where(nxt == large, -1.0, m))
         raise_to(share + 11, 0, ROWS, jnp.where(nxt == large, m, -1.0))
 
     @pl.when(has_patch)
     def _():
         patch_pair.wait_recv()
-        patch_cols = pl.multiple_of(PATCH + 128 * k, 128)
-
         def meets(start):
             t = tile(PATCH, QUARTER, pl.multiple_of(start + mine, QUARTER), QUARTER)
             s = jnp.where(start == SECOND, 4, start // ROWS)
             acc[s] = jnp.maximum(acc[s], top(t))
-            return top(tile(pl.multiple_of(start, ROWS), ROWS, patch_cols, 128))
-
-        at = pl.multiple_of(QUARTER * pick(p, PATCH_HALF) + 128 * k, 128)
+            return across(t)
+
+        at = pl.multiple_of(QUARTER * pick(p, PATCH_HALF), QUARTER)
         v = pick(p, PATCH_BLOCK)
-        here = labs[v, :, pl.ds(at, 128)] == large
+        here = labs[v, :, pl.ds(at, QUARTER)] == large
 
         def give(m):
-            raise_to(v, at, 128, jnp.where(here, m, -1.0))
-            raise_to(v + 10, at, 128, jnp.where(here, -1.0, m))
+            raise_to(v, at, QUARTER, jnp.where(here, m, -1.0))
+            raise_to(v + 10, at, QUARTER, jnp.where(here, -1.0, m))
 
         give(meets(pick(p, PATCH_MEETS)))
 
@@ -461,7 +492,7 @@
         def _():
             give(meets(jnp.int32(SLOT[2])))
 
-    for s in range(4):
+    for s in range(3):
         v = pick(p, tuple(h[s] for h in HELD))
         here = labs[v, :, pl.ds(mine, QUARTER)] == large
         raise_to(v, mine, QUARTER, jnp.where(here, acc[s], -1.0))
@@ -469,6 +500,15 @@
         @pl.when(v < 6)
         def _():
             raise_to(v + 10, mine, QUARTER, jnp.where(here, -1.0, acc[s]))
+
+    last[:, pl.ds(mine, QUARTER)] = jnp.maximum(last[:, pl.ds(mine, QUARTER)], acc[3])
+    v = pick(p, tuple(h[3] for h in HELD))
+    in_large = labs[v] == large
+    raise_to(v, 0, ROWS, jnp.where(in_large, last[...], -1.0))
+
+    @pl.when(v < 6)
+    def _():
+        raise_to(v + 10, 0, ROWS, jnp.where(in_large, -1.0, last[...]))
 
     here = labs[first, :, pl.ds(mine, QUARTER)] == large
     raise_to(second, mine, QUARTER, jnp.where(here, acc[4], -1.0))
@@ -494,7 +534,8 @@
 
     pltpu.make_async_copy(sbuf.at[0, pl.ds(0, 1008)], sbuf.at[0, pl.ds(0, 1008)], row_s).wait()
     pltpu.make_async_copy(sbuf.at[0], sbuf.at[0], row_s).wait()
-    pltpu.make_async_copy(meta_r.at[pl.ds(0, DEVS - 1)], meta_r.at[pl.ds(0, DEVS - 1)], meta_ss).wait()
+    pltpu.make_async_copy(meta_s.at[pl.ds(0, 63)], meta_s.at[pl.ds(0, 63)], meta_ss).wait()
+    meta_pair.wait_send()
     for per_bit in copies + block_pairs:
         for cp in per_bit:
             cp.wait_send()
@@ -554,15 +595,17 @@
             pltpu.VMEM((ROWS, WIDTH), BF16),
             pltpu.VMEM((2, 1024, HALF), BF16),
             pltpu.VMEM((16 * DEVS, HALF), BF16),
+            pltpu.VMEM((2 * ROWS, HALF), F32),
             pltpu.VMEM((64, 1, 128), F32),
             pltpu.VMEM((DEVS, 1, 128), F32),
             pltpu.VMEM((16, 1, ROWS), I32),
             pltpu.VMEM((2 * ROWS, 16 * DEVS), BF16),
             pltpu.VMEM((2, X_ROWS, HALF), BF16),
             pltpu.VMEM((5, 1, QUARTER), F32),
+            pltpu.VMEM((1, ROWS), F32),
             pltpu.VMEM((16, 1, ROWS), F32),
             pltpu.VMEM((16, 1, ROWS), F32),
-            dma, dma, dma, dma, dma, dma, dma, dma, dma, dma,
+            dma, dma, dma, dma, dma, dma((2,)), dma, dma, dma, dma, dma, dma,
             dma((3, len(CHUNKS))), dma((3, len(CHUNKS))), dma((n_pairs,)), dma((n_pairs,)),
             dma((2,)), dma, dma, dma, dma, dma,
         ],

time: 76.2 us -> 72.4 us (0.950)
  Pallas kernels: 74.7 us -> 71 us
    pallas_call x1, Pallas kernels: 74.7 us -> 71 us  [shards(): pl.pallas_call(kernel, out_shape=jax.ShapeDtypeStruct((1, ROWS), F32), in...]
where the time goes in v3:
time: 72.4 us; the launch traced here: 72.3 us
  Pallas kernels  71 us (98%)
  local copies, waits for them, and re-layouts  1.26 us (2%)
    pallas_call x1, Pallas kernels, shards(): pl.pallas_call(kernel, out_shape=jax.ShapeDtypeStruct((1, ROWS), F32), in...  71 us

profile of v3, /device:TPU:1, one launch (start us, length us, event | category | flops | bytes accessed | tf_op | source)
XLA Modules:
  0.0 72.3 jit_solution(247369772339144743)
XLA Ops:
  0.0 71.0 %best_match.1 = f32[1,512]{1,0:T(1,128)} custom-call(f32[512,1024]{1,0:T(8,128)} %emb_hbm.1, s32[1,512]{1,0:T(1,128)} %bitcast.1, s32[1,512]{1,0:T(1,128)} %ids_hbm.1), custom_call_target="tpu_custom_call" | custom-call | tf_op jit(solution)/shard_map/best_match/pallas_call | solution.py:582
  71.0 1.3 %copy.5 = f32[1,512]{1,0:T(1,128)} copy(f32[1,512]{1,0:T(1,128)} %best_match.1) | data formatting | bytes 4096

commit v4 on v3

--- a/solution.py
+++ b/solution.py
@@ -18,9 +18,9 @@
 VERTEX = (0, 1, 3, 7, 5, 4, 6, 2)
 HELD = ((0, 1, 9, 4), (1, 0, 2, 3), (8, 2, 0, 6), (2, 8, 1, 7), (5, 4, 6, 1), (4, 5, 3, 2), (6, 3, 5, 9), (3, 7, 4, 8))
 SLOT = (0, 512, 1024, 1536)
-SECOND, PATCH, HEAD = 2048, 2560, 2816
-HEAD_ROWS = 272
-X_ROWS = HEAD + HEAD_ROWS
+SECOND, PATCH, HEAD, TAIL = 2048, 2560, 2816, 2960
+EDGE = 144
+X_ROWS = TAIL + EDGE
 SEND = (
     (0, 0, 0, 0, 0, 0, SECOND, 0),
     (0, 0, SECOND, 0, 0, 0, 0, 0),
@@ -30,6 +30,10 @@
 PATCH_HALF = (1, 0, 0, 0, 0, 0, 1, 1)
 PATCH_MEETS = (0, 0, 0, 1536, 0, 0, SECOND, 1536)
 PATCHES = ((4, 0, 2, 256), (6, 2, 2, 1024), (6, 7, 0, 1280), (2, 3, 0, 1024), (2, 6, 2, 1280))
+MEET = (
+    ((0, 1), (0, 2), (1, 2)), ((0, 1), (0, 2), (1, 2)), ((0, 2), (0, 4), (1, 4)), ((0, 1), (0, 2), (1, 2)),
+    ((0, 1), (0, 2), (1, 2)), ((0, 1), (0, 2), (1, 2)), ((0, 1), (0, 4), (2, 4)), ((0, 1), (0, 2), (1, 2)),
+)
 CHUNKS = ((0, 128), (128, 128), (256, 128), (384, 128))
 STRIDE, INVERSE, EARLY = 45, 37, 48
 
@@ -59,10 +63,10 @@
 
 
 def kernel(
-    emb_hbm, dest_hbm, ids_hbm, out_ref,
-    emb, dest_ref, ids_ref, unit, sbuf, rb, part, meta_s, meta_r, labs, q, xs, acc, last, ob, fin,
+    emb_hbm, dest_hbm, ids_hbm, fin,
+    emb, dest_ref, ids_ref, unit, sbuf, rb, part, meta_s, meta_r, labs, q, xs, acc, last, ob,
     emb_sem, dest_sem, ids_sem, own_sem, row_s, row_r, meta_ss, meta_rr, meta_ps, meta_pr, lab_s, lab_r,
-    ici_s, ici_r, pair_s, pair_r, patch_s, patch_r, head_s, head_r, fin_s, fin_r,
+    ici_s, ici_r, pair_s, pair_r, patch_s, patch_r, edge_s, edge_r, fin_s, fin_r,
 ):
     row, col = lax.axis_index("row"), lax.axis_index("col")
     x, k, y, z = row // 2, row % 2, col // 4, col % 4
@@ -267,17 +271,21 @@
     copies = [[block_copy(bit, c) for c in range(n_chunks)] for bit in range(3)]
     block_pairs = [[pair_copy(3 + bit * n_chunks + c, SLOT[1 + bit] + CHUNKS[c][0], CHUNKS[c][1]) for c in range(n_chunks)] for bit in range(3)]
     own_pair, second_pair = pair_copy(0, 0, ROWS), pair_copy(1, SECOND, ROWS)
-    patch_pair, head_pair = pair_copy(2, PATCH, QUARTER), pair_copy(3 + 3 * n_chunks, HEAD, HEAD_ROWS)
+    patch_pair = pair_copy(2, PATCH, QUARTER)
+    head_pair, tail_pair = pair_copy(3 + 3 * n_chunks, HEAD, EDGE), pair_copy(4 + 3 * n_chunks, TAIL, EDGE)
     has_patch = (p != 1) & (p != 4) & (p != 5)
     has_head = (p != 2) & (p != 6) & (p != 4)
-    gives_head = (p != 2) & (p != 6) & (p != 0)
+    has_tail = (p != 2) & (p != 6) & (p != 0)
 
     def patch_copy(i):
         frm, to, bit, src = PATCHES[i]
         return between(src, PATCH, QUARTER, patch_s.at[i % 2], patch_r, along(bit))
 
     def head_copy(bit):
-        return between(SECOND, HEAD, HEAD_ROWS, head_s, head_r, along(bit))
+        return between(SECOND, HEAD, EDGE, edge_s.at[0], edge_r.at[0], along(bit))
+
+    def tail_copy(bit):
+        return between(SECOND + ROWS - EDGE, TAIL, EDGE, edge_s.at[1], edge_r.at[1], along(bit))
 
     def own_sends(c):
         @pl.when(p != 6)
@@ -320,13 +328,19 @@
             copies[2][c].start()
 
     second_pair.start()
-    for v, bit in ((1, 0), (3, 1), (7, 2), (5, 1), (4, 0)):
+    for v, w, bit in ((0, 1, 0), (1, 3, 1), (3, 7, 2), (7, 5, 1), (5, 4, 0)):
         @pl.when(p == v)
+        def _():
+            tail_copy(bit).start()
+
+        @pl.when(p == w)
         def _():
             head_copy(bit).start()
 
     mine = pl.multiple_of(QUARTER * k, QUARTER)
     starts = SLOT + (SECOND,)
+
+    meetings = [tuple(pick(p, tuple(m[i][side] for m in MEET)) for side in range(2)) for i in range(3)]
 
     def columns_of(s):
         return pl.multiple_of(starts[s] + mine, QUARTER)
@@ -339,11 +353,9 @@
     def top(t):
         return jnp.max(t, axis=0, keepdims=True)
 
-    def meet(s, j, nj):
-        t = tile(j, nj, columns_of(s), QUARTER)
-        if j <= starts[s] < j + nj:
-            t = jnp.where(iota((nj, QUARTER), 0) == iota((nj, QUARTER), 1) + (starts[s] - j + mine), -1.0, t)
-        acc[s] = jnp.maximum(acc[s], top(t))
+    def meet(s, other):
+        i, j = pl.multiple_of(s * ROWS + mine, QUARTER), pl.multiple_of(other * ROWS, ROWS)
+        acc[s] = jnp.maximum(acc[s], top(tile(j, ROWS, i, QUARTER)))
 
     def across(t):
         m = t[:, :128]
@@ -366,25 +378,13 @@
         def _():
             last[:, lanes] = jnp.maximum(last[:, lanes], across(against(4)))
 
-        @pl.when(k == at // QUARTER)
-        def _():
-            t = tile(rows, QUARTER, rows, QUARTER)
-            same = iota((QUARTER, QUARTER), 0) == iota((QUARTER, QUARTER), 1)
-            last[:, lanes] = jnp.maximum(last[:, lanes], top(jnp.where(same, -1.0, t)))
-
-        if at:
-            @pl.when(k == 0)
-            def _():
-                t = tile(rows, QUARTER, SLOT[3], QUARTER)
-                last[:, 0:QUARTER] = jnp.maximum(last[:, 0:QUARTER], top(t))
-                last[:, lanes] = jnp.maximum(last[:, lanes], across(t))
-
     ob[...] = jnp.full(ob.shape, -1.0, F32)
     acc[...] = jnp.full(acc.shape, -1.0, F32)
     rest_row = jnp.where(k == 0, rest_ids[:, :QUARTER], rest_ids[:, QUARTER:])
 
+    own = iota((ROWS, QUARTER), 0) == iota((ROWS, QUARTER), 1) + mine
     own_pair.wait_recv()
-    meet(0, 0, ROWS)
+    acc[0] = top(jnp.where(own, -1.0, tile(0, ROWS, columns_of(0), QUARTER)))
     for c in range(n_chunks):
         copies[0][c].wait_recv()
         copies[1][c].wait_recv()
@@ -414,60 +414,68 @@
 
     second_pair.wait_recv()
     t = tile(SECOND, ROWS, columns_of(4), QUARTER)
-    own = iota((ROWS, QUARTER), 0) == iota((ROWS, QUARTER), 1) + mine
     acc[4] = top(jnp.where((rest_col == rest_row) & jnp.logical_not(own), t, -1.0))
     for c in range(n_chunks):
         block_pairs[0][c].wait_recv()
         block_pairs[1][c].wait_recv()
-    meet(0, ROWS, 2 * ROWS)
-    meet(1, 0, 3 * ROWS)
-    meet(2, 0, 3 * ROWS)
-
-    @pl.when(large_only)
-    def _():
-        for s in range(3):
-            meet(s, SECOND, ROWS)
-        meet(4, 0, 3 * ROWS)
-
+    for a, b in meetings:
+        meet(a, b)
+        meet(b, a)
     for c in range(n_chunks - 1):
         copies[2][c].wait_recv()
         block_pairs[2][c].start()
     for c in range(n_chunks):
         if sum(CHUNKS[c]) <= QUARTER:
             block_pairs[2][c].wait_recv()
+    @pl.when(has_head)
+    def _():
+        head_copy(0).wait_recv()
+        head_pair.start()
+
+    @pl.when(has_tail)
+    def _():
+        tail_copy(0).wait_recv()
+        tail_pair.start()
+
     late(0)
     copies[2][n_chunks - 1].wait_recv()
     block_pairs[2][n_chunks - 1].start()
 
-    @pl.when(has_head)
-    def _():
-        head_copy(0).wait_recv()
-        head_pair.start()
-
     @pl.when(has_patch)
     def _():
         patch_copy(0).wait_recv()
         patch_pair.start()
+
+    def raise_to(b, at, n, v):
+        ob[b, :, pl.ds(at, n)] = jnp.maximum(ob[b, :, pl.ds(at, n)], v)
+
+    def beside(pair, start, step, at):
+        pair.wait_recv()
+        ids = labs[share + step]
+        is_here = ids == large
+        there = jnp.where(is_here, labs[share + step + 10], ids).astype(F32)
+        where = ROWS - EDGE if at else 0
+        t = tile(start, EDGE, columns_of(4), QUARTER)
+        t = jnp.where(column(there)[where : where + EDGE] == rest_row, t, -1.0)
+        acc[4] = jnp.maximum(acc[4], top(t))
+        none = jnp.full((QUARTER - EDGE, QUARTER), -1.0, F32)
+        m = across(jnp.concatenate([none, t] if at else [t, none], axis=0))
+        is_here = is_here[:, at : at + QUARTER]
+        raise_to(share + step, at, QUARTER, jnp.where(is_here, -1.0, m))
+        raise_to(share + step + 10, at, QUARTER, jnp.where(is_here, m, -1.0))
+
+    @pl.when(has_head)
+    def _():
+        beside(head_pair, HEAD, 1, 0)
+
+    @pl.when(has_tail)
+    def _():
+        beside(tail_pair, TAIL, -1, QUARTER)
 
     for c in range(n_chunks):
         if sum(CHUNKS[c]) > QUARTER:
             block_pairs[2][c].wait_recv()
     late(QUARTER)
-
-    def raise_to(b, at, n, v):
-        ob[b, :, pl.ds(at, n)] = jnp.maximum(ob[b, :, pl.ds(at, n)], v)
-
-    @pl.when(has_head)
-    def _():
-        head_pair.wait_recv()
-        nxt = labs[share + 1]
-        head_ids = jnp.where(nxt == large, labs[share + 11], nxt).astype(F32)
-        head_col = column(head_ids)[:HEAD_ROWS]
-        t = jnp.where(head_col == rest_row, tile(HEAD, HEAD_ROWS, columns_of(4), QUARTER), -1.0)
-        acc[4] = jnp.maximum(acc[4], top(t))
-        m = across(jnp.concatenate([t, jnp.full((ROWS - HEAD_ROWS, QUARTER), -1.0, F32)], axis=0))
-        raise_to(share + 1, 0, ROWS, jnp.where(nxt == large, -1.0, m))
-        raise_to(share + 11, 0, ROWS, jnp.where(nxt == large, m, -1.0))
 
     @pl.when(has_patch)
     def _():
@@ -492,24 +500,15 @@
         def _():
             give(meets(jnp.int32(SLOT[2])))
 
+    def give_block(v, at, n, m):
+        here = labs[v, :, pl.ds(at, n)] == large
+        raise_to(v, at, n, jnp.where(here, m, -1.0))
+        raise_to(jnp.minimum(v + 10, 15), at, n, jnp.where(here | (v >= 6), -1.0, m))
+
     for s in range(3):
-        v = pick(p, tuple(h[s] for h in HELD))
-        here = labs[v, :, pl.ds(mine, QUARTER)] == large
-        raise_to(v, mine, QUARTER, jnp.where(here, acc[s], -1.0))
-
-        @pl.when(v < 6)
-        def _():
-            raise_to(v + 10, mine, QUARTER, jnp.where(here, -1.0, acc[s]))
-
+        give_block(pick(p, tuple(h[s] for h in HELD)), mine, QUARTER, acc[s])
     last[:, pl.ds(mine, QUARTER)] = jnp.maximum(last[:, pl.ds(mine, QUARTER)], acc[3])
-    v = pick(p, tuple(h[3] for h in HELD))
-    in_large = labs[v] == large
-    raise_to(v, 0, ROWS, jnp.where(in_large, last[...], -1.0))
-
-    @pl.when(v < 6)
-    def _():
-        raise_to(v + 10, 0, ROWS, jnp.where(in_large, -1.0, last[...]))
-
+    give_block(pick(p, tuple(h[3] for h in HELD)), 0, ROWS, last[...])
     here = labs[first, :, pl.ds(mine, QUARTER)] == large
     raise_to(second, mine, QUARTER, jnp.where(here, acc[4], -1.0))
     raise_to(first, mine, QUARTER, jnp.where(here, -1.0, acc[4]))
@@ -545,14 +544,16 @@
     @pl.when(has_head)
     def _():
         head_pair.wait_send()
+        tail_copy(0).wait_send()
+
+    @pl.when(has_tail)
+    def _():
+        tail_pair.wait_send()
+        head_copy(0).wait_send()
 
     @pl.when(has_patch)
     def _():
         patch_pair.wait_send()
-
-    @pl.when(gives_head)
-    def _():
-        head_copy(0).wait_send()
 
     for v, which in ((4, (0,)), (6, (1, 2)), (2, (3, 4))):
         @pl.when(p == v)
@@ -571,23 +572,19 @@
         pltpu.make_async_copy(fin, fin, fin_s).wait()
 
     pltpu.make_async_copy(fin, fin, fin_r).wait()
-    best = fin[0]
-    for i in range(1, 16):
-        best = jnp.maximum(best, fin[i])
-    out_ref[...] = best
 
 
 def shards(embeddings, dest_pos, cluster_ids):
-    dma, n_pairs = pltpu.SemaphoreType.DMA, 4 + 3 * len(CHUNKS)
-    return pl.pallas_call(
+    dma, n_pairs = pltpu.SemaphoreType.DMA, 5 + 3 * len(CHUNKS)
+    bests = pl.pallas_call(
         kernel,
-        out_shape=jax.ShapeDtypeStruct((1, ROWS), F32),
+        out_shape=jax.ShapeDtypeStruct((16, 1, ROWS), F32),
         in_specs=[
             pl.BlockSpec(memory_space=pltpu.HBM),
             pl.BlockSpec(memory_space=pltpu.HBM),
             pl.BlockSpec(memory_space=pltpu.HBM),
         ],
-        out_specs=pl.BlockSpec(memory_space=pltpu.VMEM),
+        out_specs=pl.BlockSpec(memory_space=pltpu.HBM),
         scratch_shapes=[
             pltpu.VMEM((ROWS, WIDTH), F32),
             pltpu.VMEM((1, ROWS), I32),
@@ -604,16 +601,16 @@
             pltpu.VMEM((5, 1, QUARTER), F32),
             pltpu.VMEM((1, ROWS), F32),
             pltpu.VMEM((16, 1, ROWS), F32),
-            pltpu.VMEM((16, 1, ROWS), F32),
             dma, dma, dma, dma, dma, dma((2,)), dma, dma, dma, dma, dma, dma,
             dma((3, len(CHUNKS))), dma((3, len(CHUNKS))), dma((n_pairs,)), dma((n_pairs,)),
-            dma((2,)), dma, dma, dma, dma, dma,
+            dma((2,)), dma, dma((2,)), dma((2,)), dma, dma,
         ],
         compiler_params=pltpu.CompilerParams(
             collective_id=0, has_side_effects=True, vmem_limit_bytes=62 * 2**20
         ),
         name="best_match",
     )(embeddings, dest_pos.reshape(1, ROWS), cluster_ids)
+    return jnp.max(bests, axis=0)
 
 
 def solution(mesh):

time: 72.4 us -> 70.8 us (0.978)
  Pallas kernels: 71 us -> 69.2 us
  other arithmetic: 0 us -> 1.37 us
  local copies, waits for them, and re-layouts: 1.26 us -> 0 us
    pallas_call x1, Pallas kernels: 71 us -> 69.2 us  [shards(): pl.pallas_call(kernel, out_shape=jax.ShapeDtypeStruct((16, 1, ROWS), F32)...]
    reduce_max x0 -> x1, other arithmetic: none -> 1.37 us  [shards(): return jnp.max(bests, axis=0)]
    unnamed x1 -> x0, local copies, waits for them, and re-layouts: 1.26 us -> none
where the time goes in v4:
time: 70.8 us; the launch traced here: 70.6 us
  Pallas kernels  69.2 us (98%)
  other arithmetic  1.37 us (2%)
    pallas_call x1, Pallas kernels, shards(): pl.pallas_call(kernel, out_shape=jax.ShapeDtypeStruct((16, 1, ROWS), F32)...  69.2 us

profile of v4, /device:TPU:1, one launch (start us, length us, event | category | flops | bytes accessed | tf_op | source)
XLA Modules:
  0.0 70.6 jit_solution(2437194679498494473)
XLA Ops:
  0.0 69.2 %best_match.1 = f32[16,1,512]{2,1,0:T(1,128)} custom-call(f32[512,1024]{1,0:T(8,128)} %emb_hbm.1, s32[1,512]{1,0:T(1,128)} %bitcast.2, s32[1,512]{1,0:T(1,128)} %ids_hbm.1), custom_call_target="tpu_custom_call" | custom-call | tf_op jit(solution)/shard_map/best_match/pallas_call | solution.py:579
  69.2 1.4 %reduce_max.11 = f32[512]{0:T(512)} reduce(f32[16,1,512]{2,1,0:T(1,128)} %best_match.1, f32[]{:T(128)} %constant.0.clone.1), dimensions={0,1}, to_apply=%region_0.0 | reduce | flops 7680 | bytes 34820 | tf_op jit(solution)/shard_map/reduce_max | solution.py:613

commit v5 on v4

--- a/solution.py
+++ b/solution.py
@@ -92,11 +92,11 @@
     def greet(tx, ty, tz, tk):
         pl.semaphore_signal(barrier, inc=1, device_id=(2 * tx + tk, 4 * ty + tz), device_id_type=MESH)
 
-    lead = (x % 2 == 0) & (y % 2 == 0) & (z % 2 == 0)
+    lead = (x % 2 == 0) & (y % 2 == 1) & (z % 2 == 0)
 
     @pl.when(jnp.logical_not(lead & (k == 0)))
     def _():
-        greet(x - x % 2, y - y % 2, z - z % 2, 0)
+        greet(x - x % 2, y - y % 2 + 1, z - z % 2, 0)
 
     dest_copy.wait()
     dest = dest_ref[...]
@@ -148,7 +148,7 @@
     def _():
         pl.semaphore_wait(barrier, 8)
         for j in range(15, 0, -1):
-            greet(x + j // 8, y + j // 4 % 2, z + j // 2 % 2, (1 + j) % 2)
+            greet(x + j // 8, y - j // 4 % 2, z + j // 2 % 2, (1 + j) % 2)
 
     @pl.when(jnp.logical_not(lead))
     def _():
@@ -230,6 +230,15 @@
     rest_ids = jnp.where(is_large, labs[second], labs[first]).astype(F32)
     rest_col = column(rest_ids)
     large_col = column(jnp.where(is_large, 1.0, 0.0))
+
+    def beside_ids(c):
+        is_here = labs[c] == large
+        return is_here, column(jnp.where(is_here, labs[c + 10], labs[c]).astype(F32))
+
+    is_next, next_col = beside_ids(jnp.minimum(share + 1, 5))
+    is_prev, prev_col = beside_ids(jnp.clip(share - 1, 0, 5))
+    next_col, prev_col = next_col[:EDGE], prev_col[ROWS - EDGE :]
+
     index_col = iota((ROWS, 1), 0).astype(F32) + 1.0
     key_large = index_col + 512.0 * (1.0 - large_col)
     key_rest = index_col + 512.0 * large_col
@@ -449,14 +458,9 @@
     def raise_to(b, at, n, v):
         ob[b, :, pl.ds(at, n)] = jnp.maximum(ob[b, :, pl.ds(at, n)], v)
 
-    def beside(pair, start, step, at):
+    def beside(pair, start, step, at, is_here, there_col):
         pair.wait_recv()
-        ids = labs[share + step]
-        is_here = ids == large
-        there = jnp.where(is_here, labs[share + step + 10], ids).astype(F32)
-        where = ROWS - EDGE if at else 0
-        t = tile(start, EDGE, columns_of(4), QUARTER)
-        t = jnp.where(column(there)[where : where + EDGE] == rest_row, t, -1.0)
+        t = jnp.where(there_col == rest_row, tile(start, EDGE, columns_of(4), QUARTER), -1.0)
         acc[4] = jnp.maximum(acc[4], top(t))
         none = jnp.full((QUARTER - EDGE, QUARTER), -1.0, F32)
         m = across(jnp.concatenate([none, t] if at else [t, none], axis=0))
@@ -466,11 +470,11 @@
 
     @pl.when(has_head)
     def _():
-        beside(head_pair, HEAD, 1, 0)
+        beside(head_pair, HEAD, 1, 0, is_next, next_col)
 
     @pl.when(has_tail)
     def _():
-        beside(tail_pair, TAIL, -1, QUARTER)
+        beside(tail_pair, TAIL, -1, QUARTER, is_prev, prev_col)
 
     for c in range(n_chunks):
         if sum(CHUNKS[c]) > QUARTER:

time: 70.8 us -> 70.2 us (level)
  no operation moved by 1% of the time
where the time goes in v5:
time: 70.2 us; the launch traced here: 70 us
  Pallas kernels  68.6 us (98%)
  other arithmetic  1.37 us (2%)
    pallas_call x1, Pallas kernels, shards(): pl.pallas_call(kernel, out_shape=jax.ShapeDtypeStruct((16, 1, ROWS), F32)...  68.6 us

profile of v5, /device:TPU:1, one launch (start us, length us, event | category | flops | bytes accessed | tf_op | source)
XLA Modules:
  0.0 70.0 jit_solution(15413195968228347340)
XLA Ops:
  0.0 68.6 %best_match.1 = f32[16,1,512]{2,1,0:T(1,128)} custom-call(f32[512,1024]{1,0:T(8,128)} %emb_hbm.1, s32[1,512]{1,0:T(1,128)} %bitcast.2, s32[1,512]{1,0:T(1,128)} %ids_hbm.1), custom_call_target="tpu_custom_call" | custom-call | tf_op jit(solution)/shard_map/best_match/pallas_call | solution.py:583
  68.6 1.4 %reduce_max.11 = f32[512]{0:T(512)} reduce(f32[16,1,512]{2,1,0:T(1,128)} %best_match.1, f32[]{:T(128)} %constant.0.clone.1), dimensions={0,1}, to_apply=%region_0.0 | reduce | flops 7680 | bytes 34820 | tf_op jit(solution)/shard_map/reduce_max | solution.py:617

commit v6 on v5

--- a/solution.py
+++ b/solution.py
@@ -72,7 +72,8 @@
     x, k, y, z = row // 2, row % 2, col // 4, col % 4
     chip = x * 16 + y * 4 + z
     group = 2 * x + y // 2
-    p = (y % 2) * 4 + (z // 2) * 2 + (z // 2 + z) % 2
+    turned = (z + 2) % 4
+    p = (y + 1) % 2 * 4 + (turned // 2) * 2 + (turned // 2 + turned) % 2
     share = pick(p, CHIP)
     large_only = (p == 2) | (p == 6)
 
@@ -107,8 +108,8 @@
     half = jnp.where(b < 6, 0, jnp.where(b < 10, b & 1, 1))
     vert = pick(to, VERTEX)
     tx = lax.shift_right_logical(g, 1)
-    ty = 2 * (g & 1) + lax.shift_right_logical(vert, 2)
-    tz = (vert & 2) + (lax.shift_right_logical(vert, 1) + vert & 1)
+    ty = 2 * (g & 1) + (lax.shift_right_logical(vert, 2) + 1 & 1)
+    tz = (vert & 2) + (lax.shift_right_logical(vert, 1) + vert & 1) + 2 & 3
     tchip = tx * 16 + ty * 4 + tz
     turn = (((tx - x) & 3) * 16 + ((ty - y) & 3) * 4 + ((tz - z) & 3)) * INVERSE & 3
     tb = tchip * 2 + half
@@ -259,7 +260,8 @@
 
     def along(bit):
         ny = y + 1 - 2 * (y % 2) if bit == 2 else y
-        nz = z + 1 - 2 * (z % 2) if bit == 0 else 3 - z if bit == 1 else z
+        nz = turned + 1 - 2 * (turned % 2) if bit == 0 else 3 - turned if bit == 1 else turned
+        nz = (nz + 2) % 4
         return (2 * x + k, 4 * ny + nz)
 
     def between(src, dst, n, send, recv, device):

time: 70.2 us -> 69 us (0.983)
  Pallas kernels: 68.6 us -> 67.4 us
    pallas_call x1, Pallas kernels: 68.6 us -> 67.4 us  [shards(): pl.pallas_call(kernel, out_shape=jax.ShapeDtypeStruct((16, 1, ROWS), F32)...]
where the time goes in v6:
time: 69 us; the launch traced here: 68.8 us
  Pallas kernels  67.4 us (98%)
  other arithmetic  1.37 us (2%)
    pallas_call x1, Pallas kernels, shards(): pl.pallas_call(kernel, out_shape=jax.ShapeDtypeStruct((16, 1, ROWS), F32)...  67.4 us

profile of v6, /device:TPU:1, one launch (start us, length us, event | category | flops | bytes accessed | tf_op | source)
XLA Modules:
  0.0 68.8 jit_solution(15238093191647140282)
XLA Ops:
  0.0 67.4 %best_match.1 = f32[16,1,512]{2,1,0:T(1,128)} custom-call(f32[512,1024]{1,0:T(8,128)} %emb_hbm.1, s32[1,512]{1,0:T(1,128)} %bitcast.2, s32[1,512]{1,0:T(1,128)} %ids_hbm.1), custom_call_target="tpu_custom_call" | custom-call | tf_op jit(solution)/shard_map/best_match/pallas_call | solution.py:585
  67.4 1.4 %reduce_max.11 = f32[512]{0:T(512)} reduce(f32[16,1,512]{2,1,0:T(1,128)} %best_match.1, f32[]{:T(128)} %constant.0.clone.1), dimensions={0,1}, to_apply=%region_0.0 | reduce | flops 7680 | bytes 34820 | tf_op jit(solution)/shard_map/reduce_max | solution.py:619

commit v7 on v6

--- a/solution.py
+++ b/solution.py
@@ -320,11 +320,9 @@
         rows = slice(at, at + n)
         return (part[rows, :] + dot(q[rows, early:], rb[early:, :])).astype(BF16)
 
-    for at in range(0, ROWS, QUARTER):
-        xs[k, pl.ds(at, QUARTER), :] = unpacked(at, QUARTER)
-        for c in range(n_chunks):
-            if at <= CHUNKS[c][0] < at + QUARTER:
-                own_sends(c)
+    xs[k, pl.ds(0, ROWS), :] = unpacked(0, ROWS)
+    for c in range(n_chunks):
+        own_sends(c)
 
     own_pair.start()
     xs[k, pl.ds(SECOND, ROWS), :] = unpacked(ROWS, ROWS)
@@ -490,7 +488,7 @@
             t = tile(PATCH, QUARTER, pl.multiple_of(start + mine, QUARTER), QUARTER)
             s = jnp.where(start == SECOND, 4, start // ROWS)
             acc[s] = jnp.maximum(acc[s], top(t))
-            return across(t)
+            return t
 
         at = pl.multiple_of(QUARTER * pick(p, PATCH_HALF), QUARTER)
         v = pick(p, PATCH_BLOCK)
@@ -500,11 +498,15 @@
             raise_to(v, at, QUARTER, jnp.where(here, m, -1.0))
             raise_to(v + 10, at, QUARTER, jnp.where(here, -1.0, m))
 
-        give(meets(pick(p, PATCH_MEETS)))
+        t = meets(pick(p, PATCH_MEETS))
+
+        @pl.when(p != 2)
+        def _():
+            give(across(t))
 
         @pl.when(p == 2)
         def _():
-            give(meets(jnp.int32(SLOT[2])))
+            give(across(jnp.maximum(t, meets(jnp.int32(SLOT[2])))))
 
     def give_block(v, at, n, m):
         here = labs[v, :, pl.ds(at, n)] == large

time: 69 us -> 69.1 us (level)
  no operation moved by 1% of the time
where the time goes in v7:
time: 69.1 us; the launch traced here: 68.9 us
  Pallas kernels  67.6 us (98%)
  other arithmetic  1.37 us (2%)
    pallas_call x1, Pallas kernels, shards(): pl.pallas_call(kernel, out_shape=jax.ShapeDtypeStruct((16, 1, ROWS), F32)...  67.6 us

profile of v7, /device:TPU:1, one launch (start us, length us, event | category | flops | bytes accessed | tf_op | source)
XLA Modules:
  0.0 68.9 jit_solution(9721129839825104885)
XLA Ops:
  0.0 67.6 %best_match.1 = f32[16,1,512]{2,1,0:T(1,128)} custom-call(f32[512,1024]{1,0:T(8,128)} %emb_hbm.1, s32[1,512]{1,0:T(1,128)} %bitcast.2, s32[1,512]{1,0:T(1,128)} %ids_hbm.1), custom_call_target="tpu_custom_call" | custom-call | tf_op jit(solution)/shard_map/best_match/pallas_call | solution.py:587
  67.6 1.4 %reduce_max.11 = f32[512]{0:T(512)} reduce(f32[16,1,512]{2,1,0:T(1,128)} %best_match.1, f32[]{:T(128)} %constant.0.clone.1), dimensions={0,1}, to_apply=%region_0.0 | reduce | flops 7680 | bytes 34820 | tf_op jit(solution)/shard_map/reduce_max | solution.py:621

commit v8 on v6

--- a/solution.py
+++ b/solution.py
@@ -398,9 +398,14 @@
     acc[0] = top(jnp.where(own, -1.0, tile(0, ROWS, columns_of(0), QUARTER)))
     for c in range(n_chunks):
         copies[0][c].wait_recv()
+
+        @pl.when((p == 0) | (p == 3) | (p == 4) | (p == 7))
+        def _():
+            copies[2][c].start()
+
         copies[1][c].wait_recv()
 
-        @pl.when(jnp.logical_not(large_only))
+        @pl.when((p == 1) | (p == 5))
         def _():
             copies[2][c].start()
 

time: 69 us -> 69 us (level)
  no operation moved by 1% of the time
where the time goes in v8:
time: 69 us; the launch traced here: 68.8 us
  Pallas kernels  67.4 us (98%)
  other arithmetic  1.37 us (2%)
    pallas_call x1, Pallas kernels, shards(): pl.pallas_call(kernel, out_shape=jax.ShapeDtypeStruct((16, 1, ROWS), F32)...  67.4 us

profile of v8, /device:TPU:1, one launch (start us, length us, event | category | flops | bytes accessed | tf_op | source)
XLA Modules:
  0.0 68.8 jit_solution(1336917744940583077)
XLA Ops:
  0.0 67.4 %best_match.1 = f32[16,1,512]{2,1,0:T(1,128)} custom-call(f32[512,1024]{1,0:T(8,128)} %emb_hbm.1, s32[1,512]{1,0:T(1,128)} %bitcast.2, s32[1,512]{1,0:T(1,128)} %ids_hbm.1), custom_call_target="tpu_custom_call" | custom-call | tf_op jit(solution)/shard_map/best_match/pallas_call | solution.py:590
  67.4 1.4 %reduce_max.11 = f32[512]{0:T(512)} reduce(f32[16,1,512]{2,1,0:T(1,128)} %best_match.1, f32[]{:T(128)} %constant.0.clone.1), dimensions={0,1}, to_apply=%region_0.0 | reduce | flops 7680 | bytes 34820 | tf_op jit(solution)/shard_map/reduce_max | solution.py:624
